TPU v7x, 256 devices: a whole 4x4x8 slice. The times are simulated.
256 devices in a mesh: uly: 4 (over x_lo, core), blk: 64 (over x_hi, y, z).
Axes of the slice: x: 4 (x_hi: 2, x_lo: 2; x = x_hi * 2 + x_lo), y: 4, z: 8, core: 2. Of those that a mesh axis runs over, the one named last changes fastest.
Arguments:
- image_tokens: bfloat16 [12288, 1536], P(('uly', 'blk')), may hold values from -11 to 11
- text_tokens: bfloat16 [333, 1536], replicated, may hold values from -6 to 6
- w_query_key: bfloat16 [1536, 2, 1536], P(None, None, 'uly'), may hold values from -0.21875 to 0.21875
- w_value: bfloat16 [1536, 1536], P(None, 'uly'), may hold values from -0.4375 to 0.4375
- qkv_bias: float32 [3, 1536], P(None, 'uly'), may hold values from -3 to 3
- w_text: bfloat16 [1536, 2, 1536], P(None, None, 'uly'), may hold values from -0.21875 to 0.21875
- text_bias: float32 [2, 1536], P(None, 'uly'), may hold values from -3 to 3
- w_out: bfloat16 [1536, 1536], P('uly'), may hold values from -0.15625 to 0.15625
- out_bias: float32 [1536], replicated, may hold values from -3 to 3
Outputs:
- attn_out: bfloat16 [12288, 1536], P(('uly', 'blk'))
All inputs are finite; a program needn't handle non-finite values.
Results may differ from a plain program's by a relative error of at most 0.017.
The roundings to bfloat16 on the way count: a program that leaves them out, or rounds other values in their place, can miss the bound.
Values may be sent and summed in bfloat16 or wider, within the bound.
No kernel may reach another device: no remote copies, remote signals or barrier semaphores. Data moves between devices by JAX's collectives and lax.ppermute only.
A program may use at most 128 MiB of HBM per device.

v0:
```python
import functools

import jax
import jax.numpy as jnp
from jax import lax
from jax.experimental import pallas as pl
from jax.experimental.pallas import tpu as pltpu
from jax.sharding import PartitionSpec as P

HEAD_DIM = 64
AXES = ("uly", "blk")
X, CORE, Y, Z = 4, 2, 4, 8
ONES = 16
VMEM_BYTES = 16 << 20
STATS = 32
LOG2_SCALE = 1.4426950408889634 * HEAD_DIM**-0.5
SAFE_SQUARE = 96.0**2
MASKED = -1e30
BF16, F32 = jnp.bfloat16, jnp.float32


def device_id(x, core, y, z):
    return ((x % 2) * CORE + core) * (2 * Y * Z) + (x // 2) * (Y * Z) + y * Z + z


def places():
    return [
        (x, core, y, z) for x in range(X) for core in range(CORE) for y in range(Y) for z in range(Z)
    ]


def fetch(array, dx=0, dcore=0, dy=0, dz=0):
    pairs = [
        (
            device_id((x + dx) % X, (core + dcore) % CORE, (y + dy) % Y, (z + dz) % Z),
            device_id(x, core, y, z),
        )
        for x, core, y, z in places()
    ]
    return lax.ppermute(array, AXES, pairs)


def fetch_x_low(array):
    pairs = [
        (device_id(x, core, y, z), device_id(x ^ 1, core, y, z)) for x, core, y, z in places()
    ]
    return lax.ppermute(array, AXES, pairs)


def call(kernel, out_shape, flops, *operands, exps=0, aliases=None, scratch=(), scalars=(), name=None):
    spec = pl.BlockSpec(memory_space=pltpu.VMEM)
    scalar_spec = pl.BlockSpec(memory_space=pltpu.SMEM)
    moved = sum(a.size * a.dtype.itemsize for a in operands)
    return pl.pallas_call(
        kernel,
        out_shape=out_shape,
        in_specs=[scalar_spec] * len(scalars) + [spec] * len(operands),
        out_specs=jax.tree.map(lambda _: spec, out_shape),
        input_output_aliases=aliases or {},
        scratch_shapes=scratch,
        compiler_params=pltpu.CompilerParams(vmem_limit_bytes=VMEM_BYTES),
        cost_estimate=pl.CostEstimate(flops=flops, bytes_accessed=moved, transcendentals=exps),
        name=name,
    )(*scalars, *operands)


def shape(dims, dtype):
    return jax.ShapeDtypeStruct(dims, dtype)


def halves_kernel(width, high_ref, *refs):
    parts, out_ref = refs[:-1], refs[-1]
    at = 0
    for part in parts:
        for cut in range(0, part.shape[1], 2 * width):
            low, high = part[:, cut : cut + width], part[:, cut + width : cut + 2 * width]
            out_ref[:, at : at + width] = jnp.where(high_ref[0] == 1, high, low)
            at += width


def half_row(high_ref, bias_ref, width):
    halves = [
        jnp.where(high_ref[0] == 1, bias_ref[at : at + 1, width:], bias_ref[at : at + 1, :width])
        for at in range(bias_ref.shape[0])
    ]
    return jnp.concatenate(halves, axis=1)


def project_kernel(high_ref, w_ref, bias_ref, *refs):
    blocks, (q_ref, kv_ref, tokens) = refs[:-3], refs[-3:]
    heads = q_ref.shape[0]
    width = heads * HEAD_DIM
    rows = blocks[0].shape[0]
    for at, block in enumerate(blocks):
        tokens[at * rows : (at + 1) * rows, :] = block[...]
    projected = jnp.dot(tokens[...], w_ref[...], preferred_element_type=F32)
    projected = projected + half_row(high_ref, bias_ref, width)
    columns = projected.T.astype(BF16)
    for h in range(heads):
        cut = h * HEAD_DIM
        q_ref[h] = columns[cut : cut + HEAD_DIM]
        kv_ref[h, :HEAD_DIM, :] = columns[width + cut : width + cut + HEAD_DIM]
        kv_ref[h, HEAD_DIM:, :] = columns[2 * width + cut : 2 * width + cut + HEAD_DIM]


def text_kernel(high_ref, text_ref, w_ref, bias_ref, kv_ref, rows_ref):
    heads = kv_ref.shape[0]
    width = heads * HEAD_DIM
    count = text_ref.shape[0]
    rows_ref[...] = jnp.zeros_like(rows_ref)
    rows = jnp.dot(text_ref[...], w_ref[...], preferred_element_type=F32)
    rows_ref[:count, :] = rows + half_row(high_ref, bias_ref, width)
    columns = rows_ref[...].T.astype(BF16)
    for h in range(heads):
        cut = h * HEAD_DIM
        kv_ref[h, :HEAD_DIM, :] = columns[cut : cut + HEAD_DIM]
        kv_ref[h, HEAD_DIM:, :] = columns[width + cut : width + cut + HEAD_DIM]


def scale_queries(parts, q2_ref, norm_ref):
    for h in range(q2_ref.shape[0]):
        largest = None
        for at, part in enumerate(parts):
            scaled = part[h].astype(F32) * LOG2_SCALE
            high = scaled.astype(BF16)
            low = (scaled - high.astype(F32)).astype(BF16)
            here = slice(at * part.shape[2], (at + 1) * part.shape[2])
            q2_ref[h, :HEAD_DIM, here] = high
            q2_ref[h, HEAD_DIM:, here] = low
            top = jnp.max(jnp.sum(scaled * scaled, axis=0, keepdims=True), axis=1, keepdims=True)
            largest = top if largest is None else jnp.maximum(largest, top)
        norm_ref[h] = jnp.broadcast_to(largest, norm_ref.shape[1:])


def keys_of(parts, h):
    return jnp.concatenate([k[h, :HEAD_DIM, :] for k, _ in parts], axis=1)


def values_of(parts, h, count):
    values = jnp.concatenate([v[h, -HEAD_DIM:, :] for _, v in parts], axis=1)
    ones = jnp.ones((ONES, values.shape[1]), BF16)
    if count is not None:
        inside = lax.broadcasted_iota(jnp.int32, ones.shape, 1) < count
        ones = jnp.where(inside, 1.0, 0.0).astype(BF16)
    return jnp.concatenate([values, ones], axis=0)


def attend(parts, text, q2_ref, norm_ref, bound, state_in, acc_ref, m_ref, bound_ref, tile):
    heads, _, queries = q2_ref.shape
    worst = None
    for h in range(heads):
        top = None
        for some in (parts, text[0]) if text else (parts,):
            keys = keys_of(some, h).astype(F32)
            one = jnp.max(jnp.sum(keys * keys, axis=0, keepdims=True), axis=1, keepdims=True)
            top = one if top is None else jnp.maximum(top, one)
        product = top * norm_ref[h, 0:1, 0:1]
        worst = product if worst is None else jnp.maximum(worst, product)
    if bound is not None:
        worst = jnp.maximum(worst, bound[0:1, 0:1])
    bound_ref[...] = jnp.broadcast_to(worst, bound_ref.shape)
    safe = jnp.max(worst) <= SAFE_SQUARE

    def doubled_keys(some, h):
        keys = keys_of(some, h)
        return jnp.concatenate([keys, keys], axis=0).T

    @pl.when(safe)
    def _():
        def visit(some, count, h, here, before):
            scores = jnp.dot(doubled_keys(some, h), q2_ref[h, :, here], preferred_element_type=F32)
            weights = jnp.exp2(scores).astype(BF16)
            term = jnp.dot(values_of(some, h, count), weights, preferred_element_type=F32)
            acc_ref[h, :, here] = term if before is None else before[h, :, here] + term

        for h in range(heads):
            for at in range(0, queries, tile):
                visit(parts, None, h, slice(at, at + tile), state_in and state_in[0])
            if text:
                visit(*text, h, slice(0, queries // Y), acc_ref)
        m_ref[...] = jnp.zeros_like(m_ref) if state_in is None else state_in[1][...]

    @pl.when(jnp.logical_not(safe))
    def _():
        step = 128

        def pass_over(some, count, queries, before):
            def one_head(h, carry):
                keys, values = doubled_keys(some, h), values_of(some, h, count)

                def one_tile(at, carry):
                    here = pl.ds(pl.multiple_of(at * step, step), step)
                    scores = jnp.dot(keys, q2_ref[h, :, here], preferred_element_type=F32)
                    if count is not None:
                        inside = lax.broadcasted_iota(jnp.int32, scores.shape, 0) < count
                        scores = jnp.where(inside, scores, MASKED)
                    top = jnp.max(scores, axis=0, keepdims=True)
                    if before is not None:
                        old = before[1][h, 0:1, here]
                        top = jnp.maximum(top, old)
                    weights = jnp.exp2(scores - top).astype(BF16)
                    term = jnp.dot(values, weights, preferred_element_type=F32)
                    if before is not None:
                        term = term + before[0][h, :, here] * jnp.exp2(old - top)
                    acc_ref[h, :, here] = term
                    m_ref[h, :, here] = jnp.broadcast_to(top, (m_ref.shape[1], step))
                    return carry

                return lax.fori_loop(0, queries // step, one_tile, carry)

            lax.fori_loop(0, heads, one_head, 0)

        pass_over(parts, None, queries, state_in)
        if text:
            pass_over(*text, queries // Y, (acc_ref, m_ref))


def first_kernel(n_parts, tile, *refs):
    q_refs, kv_refs = refs[:Y], refs[Y : Y + n_parts]
    acc_ref, m_ref, bound_ref, q2_ref, norm_ref = refs[Y + n_parts :]
    scale_queries(q_refs, q2_ref, norm_ref)
    parts = [(r, r) for r in kv_refs]
    attend(parts, None, q2_ref, norm_ref, None, None, acc_ref, m_ref, bound_ref, tile)


def next_kernel(n_parts, tile, count, *refs):
    kv_refs, refs = refs[:n_parts], refs[n_parts:]
    text = None
    if count:
        text, refs = ([(refs[0], refs[0])], count), refs[1:]
    q2_ref, norm_ref, acc_in, m_in, bound_in, acc_ref, m_ref, bound_ref = refs
    parts = [(r, r) for r in kv_refs]
    state = (acc_in, m_in)
    attend(parts, text, q2_ref, norm_ref, bound_in, state, acc_ref, m_ref, bound_ref, tile)


def three_parts(value):
    high = value.astype(BF16).astype(F32)
    middle = (value - high).astype(BF16).astype(F32)
    return [high, middle, value - high - middle]


def last_kernel(tile, k_ref, v_ref, *refs):
    q2_ref, norm_ref, acc_in, m_in, bound_in, own_acc, own_m = refs[:7]
    packs, (acc_ref, m_ref, bound_ref) = refs[7:-3], refs[-3:]
    parts = [(k_ref, v_ref)]
    state = (acc_in, m_in)
    attend(parts, None, q2_ref, norm_ref, bound_in, state, acc_ref, m_ref, bound_ref, tile)
    heads, _, queries = q2_ref.shape
    mine = queries // Y
    own_acc[...] = acc_ref[:, :, :mine]
    own_m[...] = m_ref[:, :, :mine]
    for at, pack in enumerate(packs):
        here = slice((at + 1) * mine, (at + 2) * mine)
        rows = []
        for h in range(heads):
            pack[h * HEAD_DIM : (h + 1) * HEAD_DIM, :] = acc_ref[h, :HEAD_DIM, here].astype(BF16)
            rows += three_parts(acc_ref[h, HEAD_DIM : HEAD_DIM + 1, here])
            rows += three_parts(m_ref[h, 0:1, here])
        rows.append(jnp.zeros((STATS - len(rows), mine), F32))
        pack[heads * HEAD_DIM :, :] = jnp.concatenate(rows, axis=0).astype(BF16)


def combine_kernel(odd_ref, acc_ref, m_ref, *refs):
    packs, (kept_ref, sent_ref) = refs[:-2], refs[-2:]
    heads, _, mine = acc_ref.shape
    columns = []
    for h in range(heads):
        sums = [acc_ref[h, :HEAD_DIM, :]]
        totals = [acc_ref[h, HEAD_DIM : HEAD_DIM + 1, :]]
        tops = [m_ref[h, 0:1, :]]
        for pack in packs:
            sums.append(pack[h * HEAD_DIM : (h + 1) * HEAD_DIM, :].astype(F32))
            stats = pack[heads * HEAD_DIM :, :].astype(F32)
            at = 6 * h
            totals.append(stats[at : at + 1] + stats[at + 1 : at + 2] + stats[at + 2 : at + 3])
            tops.append(stats[at + 3 : at + 4] + stats[at + 4 : at + 5] + stats[at + 5 : at + 6])
        top = functools.reduce(jnp.maximum, tops)
        shares = [jnp.exp2(t - top) for t in tops]
        total = sum(t * s for t, s in zip(totals, shares))
        mixed = sum(a * s for a, s in zip(sums, shares))
        columns.append(mixed / total)
    rows = jnp.concatenate(columns, axis=0).T.astype(BF16)
    block = mine // (X * CORE)
    for core in range(CORE):
        here, up, down, far = [
            rows[(core * X + at) * block : (core * X + at + 1) * block] for at in range(X)
        ]
        at = 2 * core * block
        kept_ref[at : at + block, :] = here
        sent_ref[at : at + block, :] = far
        kept_ref[at + block : at + 2 * block, :] = jnp.where(odd_ref[0] == 1, down, up)
        sent_ref[at + block : at + 2 * block, :] = jnp.where(odd_ref[0] == 1, up, down)


def out_rows(rows_ref, w_ref, half):
    width = rows_ref.shape[1]
    here = pl.ds(pl.multiple_of(half * width, width), width)
    return jnp.dot(rows_ref[...], w_ref[here, :], preferred_element_type=F32)


def near_kernel(high_ref, rows_ref, w_ref, out_ref):
    out_ref[...] = out_rows(rows_ref, w_ref, high_ref[0])


def far_kernel(high_ref, rows_ref, w_ref, near_ref, kept_ref, sent_ref):
    total = near_ref[...] + out_rows(rows_ref, w_ref, 1 - high_ref[0])
    half = kept_ref.shape[0]
    kept_ref[...] = total[:half]
    sent_ref[...] = total[half:].astype(BF16)


def add_kernel(kept_in, received_ref, kept_ref, sent_ref):
    total = kept_in[...] + received_ref[...].astype(F32)
    half = kept_ref.shape[0]
    kept_ref[...] = total[:half]
    sent_ref[...] = total[half:].astype(BF16)


def finish_kernel(kept_ref, received_ref, bias_ref, out_ref):
    out_ref[...] = (kept_ref[...] + received_ref[...].astype(F32) + bias_ref[...]).astype(BF16)


def body(
    image_tokens, text_tokens, w_query_key, w_value, qkv_bias, w_text, text_bias, w_out, out_bias
):
    block, model_width = image_tokens.shape
    local_width = w_value.shape[1]
    width = local_width // 2
    heads = width // HEAD_DIM
    mine = block * X * CORE
    queries = mine * Y
    text_count = text_tokens.shape[0]
    text_rows = -(-text_count // 128) * 128
    blk, uly = lax.axis_index("blk"), lax.axis_index("uly")
    x_high = blk // (Y * Z)
    x_at, core_at = x_high * 2 + uly // CORE, uly % CORE

    with jax.named_scope("tokens"):
        near = [image_tokens] + [fetch(image_tokens, dx=d) for d in (1, -1, 2)]

    with jax.named_scope("weights"):
        high = x_high.reshape(1).astype(jnp.int32)

        def halves(*parts):
            columns = sum(p.shape[1] for p in parts) // 2
            return call(
                functools.partial(halves_kernel, width),
                shape((model_width, columns), BF16),
                0,
                *parts,
                scalars=(high,),
                name="halves",
            )

        weights = halves(w_query_key.reshape(model_width, 2 * local_width), w_value)

    with jax.named_scope("project"):
        sibling = fetch(image_tokens, dcore=1)
        near, weights = lax.optimization_barrier((near, weights))
        blocks = near + [sibling] + [fetch(block_rows, dcore=1) for block_rows in near[1:]]
        q_own, kv_own = call(
            project_kernel,
            (shape((heads, HEAD_DIM, mine), BF16), shape((heads, 2 * HEAD_DIM, mine), BF16)),
            6 * mine * model_width * width,
            weights,
            qkv_bias,
            *blocks,
            scalars=(high,),
            scratch=[pltpu.VMEM((mine, model_width), BF16)],
            name="project",
        )
    with jax.named_scope("exchange"):
        up = [fetch(kv_own, dz=1)]
        down = [fetch(kv_own, dz=-1)]
        w_text, up[0] = lax.optimization_barrier((w_text, up[0]))
        text_kv = call(
            text_kernel,
            shape((heads, 2 * HEAD_DIM, text_rows), BF16),
            4 * text_rows * model_width * width,
            text_tokens,
            halves(w_text.reshape(model_width, 2 * local_width)),
            text_bias,
            scalars=(high,),
            scratch=[pltpu.VMEM((text_rows, 2 * width), F32)],
            name="text_project",
        )
        q_parts = [q_own] + [fetch(q_own, dy=d) for d in (1, -1, 2)]
        for _ in range(2):
            up.append(fetch(up[-1], dz=1))
            down.append(fetch(down[-1], dz=-1))
        far_keys = fetch(up[-1][:, :HEAD_DIM], dz=1)
        far_values = fetch(down[-1][:, HEAD_DIM:], dz=-1)

    def state_shapes(count):
        return (
            shape((heads, HEAD_DIM + ONES, count), F32),
            shape((heads, 8, count), F32),
            shape((8, 128), F32),
        )

    def query_shapes(count):
        return (shape((heads, 2 * HEAD_DIM, count), BF16), shape((heads, 8, 128), F32))

    def costs(rows, columns):
        return 2500 * heads * rows * columns

    with jax.named_scope("attend"):
        acc, m, bound, q2, norm = call(
            functools.partial(first_kernel, 3, 768),
            state_shapes(queries) + query_shapes(queries),
            costs(queries, 3 * mine),
            *q_parts,
            kv_own,
            up[0],
            down[0],
            exps=0,
            name="attend_first",
        )
        for at in (1, 2):
            extra = [text_kv] if at == 1 else []
            acc, m, bound = call(
                functools.partial(next_kernel, 2, 768, text_count if extra else None),
                state_shapes(queries),
                costs(queries, 2 * mine),
                up[at],
                down[at],
                *extra,
                q2,
                norm,
                acc,
                m,
                bound,
                exps=0,
                aliases={n + 4 + len(extra): n for n in range(3)},
                name="attend_next",
            )
        pack = shape((heads * HEAD_DIM + STATS, mine), BF16)
        acc, m, *packs = call(
            functools.partial(last_kernel, 1536),
            state_shapes(mine)[:2] + (pack,) * (Y - 1),
            costs(queries, mine),
            far_keys,
            far_values,
            q2,
            norm,
            acc,
            m,
            bound,
            exps=0,
            scratch=[pltpu.VMEM(s.shape, s.dtype) for s in state_shapes(queries)],
            name="attend_last",
        )

    with jax.named_scope("combine"):
        returned = [fetch(pack, dy=-d) for pack, d in zip(packs, (1, -1, 2))]
        rows = shape((mine // 2, width), BF16)
        odd = (x_at % 2).reshape(1).astype(jnp.int32)
        kept, sent = call(
            combine_kernel, (rows, rows), 0, acc, m, *returned, scalars=(odd,), name="combine"
        )

    with jax.named_scope("output"):
        received = fetch(sent, dx=2)
        flops = mine * width * model_width
        near_sum = call(
            near_kernel,
            shape((mine // 2, model_width), F32),
            flops,
            kept,
            w_out,
            scalars=(high,),
            name="output_near",
        )
        received, near_sum = lax.optimization_barrier((received, near_sum))

        def split(rows):
            return (shape((rows, model_width), F32), shape((rows, model_width), BF16))

        kept, sent = call(
            far_kernel,
            split(mine // 4),
            flops,
            received,
            w_out,
            near_sum,
            scalars=(high,),
            name="output_far",
        )
        kept, sent = call(add_kernel, split(block), 0, kept, fetch(sent, dcore=1), name="add_cores")
        return call(
            finish_kernel,
            shape((block, model_width), BF16),
            0,
            kept,
            fetch_x_low(sent),
            out_bias.reshape(1, -1),
            name="finish",
        )


def solution(mesh):
    in_specs = (
        P(("uly", "blk"), None),
        P(),
        P(None, None, "uly"),
        P(None, "uly"),
        P(None, "uly"),
        P(None, None, "uly"),
        P(None, "uly"),
        P("uly", None),
        P(),
    )
    out_specs = P(("uly", "blk"), None)
    return jax.shard_map(body, mesh=mesh, in_specs=in_specs, out_specs=out_specs, check_vma=False)
```

profile of v0, /device:TPU:1, one launch (start us, length us, event | category | flops | bytes accessed | tf_op | source)
XLA Modules:
  0.0 143.6 jit_solution(1157745358024594993)
XLA Ops:
  0.0 3.3 %collective-permute-start = (bf16[48,1536]{1,0:T(8,128)(2,1)}, bf16[48,1536]{1,0:T(8,128)(2,1)}, u32[]{:S(2)}, u32[]{:S(2)}) collective-permute-start(bf16[48,1536]{1,0:T(8,128)(2,1)} %refs_0_), channel_id=1, source_target_pairs={{128,0},{129,1},{130,2},{131,3},{132,4},{133,5},{134,6},{135,7},{1... | collective-permute-start | bytes 442376 | tf_op jit(solution)/shard_map/tokens/ppermute | solution.py:40
  3.3 1.7 %collective-permute-start.2 = (bf16[48,1536]{1,0:T(8,128)(2,1)}, bf16[48,1536]{1,0:T(8,128)(2,1)}, u32[]{:S(2)}, u32[]{:S(2)}) collective-permute-start(bf16[48,1536]{1,0:T(8,128)(2,1)} %refs_0_), channel_id=1, source_target_pairs={{32,0},{33,1},{34,2},{35,3},{36,4},{37,5},{38,6},{39,7},{40,8},{41... | collective-permute-start | bytes 442376 | tf_op jit(solution)/shard_map/tokens/ppermute | solution.py:40
  5.0 1.5 %collective-permute-start.3 = (bf16[48,1536]{1,0:T(8,128)(2,1)}, bf16[48,1536]{1,0:T(8,128)(2,1)}, u32[]{:S(2)}, u32[]{:S(2)}) collective-permute-start(bf16[48,1536]{1,0:T(8,128)(2,1)} %refs_0_), channel_id=1, source_target_pairs={{64,0},{65,1},{66,2},{67,3},{68,4},{69,5},{70,6},{71,7},{72,8},{73... | collective-permute-start | bytes 442376 | tf_op jit(solution)/shard_map/project/ppermute | solution.py:40
  6.6 2.2 %copy.16 = bf16[192,8,2,384]{3,1,2,0:T(8,128)(2,1)S(1)} copy(bf16[192,8,2,384]{3,2,1,0:T(2,128)(2,1)} %bitcast.8) | data formatting | bytes 4718592
  11.4 2.8 %collective-permute-start.4 = (bf16[48,1536]{1,0:T(8,128)(2,1)}, bf16[48,1536]{1,0:T(8,128)(2,1)S(1)}, u32[]{:S(2)}, u32[]{:S(2)}) collective-permute-start(bf16[48,1536]{1,0:T(8,128)(2,1)} %collective-permute-done.refs_1_), channel_id=1, source_target_pairs={{64,0},{65,1},{66,2},{67,3},{68,4},{69,5},{70,6},{71,7},{72,8},{73... | collective-permute-start | bytes 442376 | tf_op jit(solution)/shard_map/project/ppermute | solution.py:40
  16.1 2.3 %project.1 = (bf16[3,64,384]{2,1,0:T(8,128)(2,1)S(1)}, bf16[3,128,384]{2,1,0:T(8,128)(2,1)S(1)}) custom-call(s32[1]{0:T(128)} %bitcast.high_ref, bf16[1536,576]{1,0:T(8,128)(2,1)S(1)} %halves.2.w_ref, f32[3,384]{1,0:T(4,128)S(1)} %copy-done.4, bf16[48,1536]{1,0:T(8,128)(2,1)S(1)} %copy-done.3, bf16[48,1536]{1,0:T(8,128)(2,1)} %collective-permute-done.refs_1_, ...), custom_call_target="tpu_custom_call" | custom-call | flops 679477248 | bytes 2953728 | tf_op jit(solution)/shard_map/project/project/pallas_call | solution.py:54
  18.4 5.7 %collective-permute-start.7 = (bf16[3,128,384]{2,1,0:T(8,128)(2,1)S(1)}, bf16[3,128,384]{2,1,0:T(8,128)(2,1)S(1)}, u32[]{:S(2)}, u32[]{:S(2)}) collective-permute-start(bf16[3,128,384]{2,1,0:T(8,128)(2,1)S(1)} %get-tuple-element.43.refs_4_), channel_id=1, source_target_pairs={{1,0},{2,1},{3,2},{4,3},{5,4},{6,5},{7,6},{0,7},{9,8},{10,9},{11,1... | collective-permute-start | bytes 884744 | tf_op jit(solution)/shard_map/exchange/ppermute | solution.py:40
  24.0 2.7 %collective-permute-start.15 = (bf16[3,64,384]{2,1,0:T(8,128)(2,1)S(1)}, bf16[3,64,384]{2,1,0:T(8,128)(2,1)S(1)}, u32[]{:S(2)}, u32[]{:S(2)}) collective-permute-start(bf16[3,64,384]{2,1,0:T(8,128)(2,1)S(1)} %get-tuple-element.45.refs_0_), channel_id=1, source_target_pairs={{8,0},{9,1},{10,2},{11,3},{12,4},{13,5},{14,6},{15,7},{16,8},{17,9... | collective-permute-start | bytes 442376 | tf_op jit(solution)/shard_map/exchange/ppermute | solution.py:40
  26.8 1.6 %collective-permute-start.17 = (bf16[3,64,384]{2,1,0:T(8,128)(2,1)S(1)}, bf16[3,64,384]{2,1,0:T(8,128)(2,1)S(1)}, u32[]{:S(2)}, u32[]{:S(2)}) collective-permute-start(bf16[3,64,384]{2,1,0:T(8,128)(2,1)S(1)} %get-tuple-element.45.refs_0_), channel_id=1, source_target_pairs={{16,0},{17,1},{18,2},{19,3},{20,4},{21,5},{22,6},{23,7},{24,8},{25... | collective-permute-start | bytes 442376 | tf_op jit(solution)/shard_map/exchange/ppermute | solution.py:40
  28.4 1.7 %collective-permute-done.7.refs_5_ = bf16[3,128,384]{2,1,0:T(8,128)(2,1)S(1)} collective-permute-done((bf16[3,128,384]{2,1,0:T(8,128)(2,1)S(1)}, bf16[3,128,384]{2,1,0:T(8,128)(2,1)S(1)}, u32[]{:S(2)}, u32[]{:S(2)}) %collective-permute-start.7) | collective-permute-done | bytes 294944 | tf_op jit(solution)/shard_map/exchange/ppermute | solution.py:40
  30.1 3.4 %collective-permute-start.8 = (bf16[3,128,384]{2,1,0:T(8,128)(2,1)S(1)}, bf16[3,128,384]{2,1,0:T(8,128)(2,1)S(1)}, u32[]{:S(2)}, u32[]{:S(2)}) collective-permute-start(bf16[3,128,384]{2,1,0:T(8,128)(2,1)S(1)} %collective-permute-done.7.refs_5_), channel_id=1, source_target_pairs={{1,0},{2,1},{3,2},{4,3},{5,4},{6,5},{7,6},{0,7},{9,8},{10,9},{11,1... | collective-permute-start | bytes 884744 | tf_op jit(solution)/shard_map/exchange/ppermute | solution.py:40
  34.6 20.5 %attend_first.1 = (f32[3,80,1536]{2,1,0:T(8,128)S(1)}, f32[3,8,1536]{2,1,0:T(8,128)S(1)}, f32[8,128]{1,0:T(8,128)S(1)}, bf16[3,128,1536]{2,1,0:T(8,128)(2,1)S(1)}, f32[3,8,128]{2,1,0:T(8,128)S(1)}) custom-call(bf16[3,64,384]{2,1,0:T(8,128)(2,1)S(1)} %get-tuple-element.45.refs_0_, bf16[3,64,384]{2,1,0:T(8,128)(2,1)S(1)} %collective-permute-done.15.refs_1_, ...), custom_call_target="tpu_custom_call" | custom-call | flops 13271040000 | bytes 1474560 | tf_op jit(solution)/shard_map/attend/attend_first/pallas_call | solution.py:54
  57.6 2.5 %collective-permute-start.9 = (bf16[3,128,384]{2,1,0:T(8,128)(2,1)S(1)}, bf16[3,128,384]{2,1,0:T(8,128)(2,1)S(1)}, u32[]{:S(2)}, u32[]{:S(2)}) collective-permute-start(bf16[3,128,384]{2,1,0:T(8,128)(2,1)S(1)} %collective-permute-done.8.refs_0_), channel_id=1, source_target_pairs={{1,0},{2,1},{3,2},{4,3},{5,4},{6,5},{7,6},{0,7},{9,8},{10,9},{11,1... | collective-permute-start | bytes 884744 | tf_op jit(solution)/shard_map/exchange/ppermute | solution.py:40
  60.1 20.9 %attend_next.2 = (f32[3,80,1536]{2,1,0:T(8,128)S(1)}, f32[3,8,1536]{2,1,0:T(8,128)S(1)}, f32[8,128]{1,0:T(8,128)S(1)}) custom-call(bf16[3,128,384]{2,1,0:T(8,128)(2,1)S(1)} %collective-permute-done.8.refs_0_, bf16[3,128,384]{2,1,0:T(8,128)(2,1)S(1)} %collective-permute-done.12.refs_1_, ...), custom_call_target="tpu_custom_call", output_to_operand_aliasing={{0}: (5, {}), {1}: (6, {}), {2}: (7, {})} | custom-call | flops 8847360000 | bytes 3702784 | tf_op jit(solution)/shard_map/attend/attend_next/pallas_call | solution.py:54
  81.0 2.8 %collective-permute-start.10 = (bf16[3,64,384]{2,1,0:T(8,128)(2,1)S(1)}, bf16[3,64,384]{2,1,0:T(8,128)(2,1)S(1)}, u32[]{:S(2)}, u32[]{:S(2)}) collective-permute-start(bf16[3,64,384]{2,1,0:T(8,128)(2,1)S(1)} %slice.8), channel_id=1, source_target_pairs={{1,0},{2,1},{3,2},{4,3},{5,4},{6,5},{7,6},{0,7},{9,8},{10,9},{11,1... | collective-permute-start | bytes 442376 | tf_op jit(solution)/shard_map/exchange/ppermute | solution.py:40
  83.9 16.9 %attend_next.3 = (f32[3,80,1536]{2,1,0:T(8,128)S(1)}, f32[3,8,1536]{2,1,0:T(8,128)S(1)}, f32[8,128]{1,0:T(8,128)S(1)}) custom-call(bf16[3,128,384]{2,1,0:T(8,128)(2,1)S(1)} %collective-permute-done.9.refs_0_, bf16[3,128,384]{2,1,0:T(8,128)(2,1)S(1)} %collective-permute-done.13.refs_1_, ...), custom_call_target="tpu_custom_call", output_to_operand_aliasing={{0}: (4, {}), {1}: (5, {}), {2}: (6, {})} | custom-call | flops 8847360000 | bytes 3407872 | tf_op jit(solution)/shard_map/attend/attend_next/pallas_call | solution.py:54
  100.9 14.5 %attend_last.1 = (f32[3,80,384]{2,1,0:T(8,128)S(1)}, f32[3,8,384]{2,1,0:T(8,128)S(1)}, bf16[224,384]{1,0:T(8,128)(2,1)S(1)}, bf16[224,384]{1,0:T(8,128)(2,1)S(1)}, bf16[224,384]{1,0:T(8,128)(2,1)S(1)}) custom-call(bf16[3,64,384]{2,1,0:T(8,128)(2,1)S(1)} %collective-permute-done.10.k_ref, bf16[3,64,384]{2,1,0:T(8,128)(2,1)S(1)} %collective-permute-done.14.v_ref, ...), custom_call_target="tpu_custom_call" | custom-call | flops 4423680000 | bytes 3112960 | tf_op jit(solution)/shard_map/attend/attend_last/pallas_call | solution.py:54
  116.0 2.1 %collective-permute-start.19 = (bf16[224,384]{1,0:T(8,128)(2,1)S(1)}, bf16[224,384]{1,0:T(8,128)(2,1)S(1)}, u32[]{:S(2)}, u32[]{:S(2)}) collective-permute-start(bf16[224,384]{1,0:T(8,128)(2,1)S(1)} %get-tuple-element.61), channel_id=1, source_target_pairs={{8,0},{9,1},{10,2},{11,3},{12,4},{13,5},{14,6},{15,7},{16,8},{17,9... | collective-permute-start | bytes 516104 | tf_op jit(solution)/shard_map/combine/ppermute | solution.py:40
  119.1 1.8 %collective-permute-done.18.refs_0_ = bf16[224,384]{1,0:T(8,128)(2,1)S(1)} collective-permute-done((bf16[224,384]{1,0:T(8,128)(2,1)S(1)}, bf16[224,384]{1,0:T(8,128)(2,1)S(1)}, u32[]{:S(2)}, u32[]{:S(2)}) %collective-permute-start.18) | collective-permute-done | bytes 172064 | tf_op jit(solution)/shard_map/combine/ppermute | solution.py:40
  121.0 1.4 collective-permute-done.19.refs_1_
  122.4 3.0 %collective-permute-done.20.refs_2_ = bf16[224,384]{1,0:T(8,128)(2,1)S(1)} collective-permute-done((bf16[224,384]{1,0:T(8,128)(2,1)S(1)}, bf16[224,384]{1,0:T(8,128)(2,1)S(1)}, u32[]{:S(2)}, u32[]{:S(2)}) %collective-permute-start.20) | collective-permute-done | bytes 172064 | tf_op jit(solution)/shard_map/combine/ppermute | solution.py:40
  126.4 4.3 %collective-permute-done.21.rows_ref = bf16[192,192]{1,0:T(8,128)(2,1)S(1)} collective-permute-done((bf16[192,192]{1,0:T(8,128)(2,1)S(1)}, bf16[192,192]{1,0:T(8,128)(2,1)S(1)}, u32[]{:S(2)}, u32[]{:S(2)}) %collective-permute-start.21) | collective-permute-done | bytes 73760 | tf_op jit(solution)/shard_map/output/ppermute | solution.py:40
  131.0 5.4 %collective-permute-start.22 = (bf16[96,1536]{1,0:T(8,128)(2,1)S(1)}, bf16[96,1536]{1,0:T(8,128)(2,1)S(1)}, u32[]{:S(2)}, u32[]{:S(2)}) collective-permute-start(bf16[96,1536]{1,0:T(8,128)(2,1)S(1)} %get-tuple-element.68), channel_id=1, source_target_pairs={{64,0},{65,1},{66,2},{67,3},{68,4},{69,5},{70,6},{71,7},{72,8},{73... | collective-permute-start | bytes 884744 | tf_op jit(solution)/shard_map/output/ppermute | solution.py:40
  137.9 5.0 %collective-permute-done.23.received_ref = bf16[48,1536]{1,0:T(8,128)(2,1)S(1)} collective-permute-done((bf16[48,1536]{1,0:T(8,128)(2,1)S(1)}, bf16[48,1536]{1,0:T(8,128)(2,1)S(1)}, u32[]{:S(2)}, u32[]{:S(2)}) %collective-permute-start.23) | collective-permute-done | bytes 147488 | tf_op jit(solution)/shard_map/output/ppermute | solution.py:47
  (58 shorter events, 13.1 us)
Async XLA Ops:
  0.0 9.9 %collective-permute-start = (bf16[48,1536]{1,0:T(8,128)(2,1)}, bf16[48,1536]{1,0:T(8,128)(2,1)}, u32[]{:S(2)}, u32[]{:S(2)}) collective-permute-start(bf16[48,1536]{1,0:T(8,128)(2,1)} %refs_0_), channel_id=1, source_target_pairs={{128,0},{129,1},{130,2},{131,3},{132,4},{133,5},{134,6},{135,7},{1... | collective-permute-start | bytes 442376 | tf_op jit(solution)/shard_map/tokens/ppermute | solution.py:40
  3.3 7.5 %collective-permute-start.1 = (bf16[48,1536]{1,0:T(8,128)(2,1)}, bf16[48,1536]{1,0:T(8,128)(2,1)}, u32[]{:S(2)}, u32[]{:S(2)}) collective-permute-start(bf16[48,1536]{1,0:T(8,128)(2,1)} %refs_0_), channel_id=1, source_target_pairs={{160,0},{161,1},{162,2},{163,3},{164,4},{165,5},{166,6},{167,7},{1... | collective-permute-start | bytes 442376 | tf_op jit(solution)/shard_map/tokens/ppermute | solution.py:40
  3.3 8.1 %collective-permute-start.2 = (bf16[48,1536]{1,0:T(8,128)(2,1)}, bf16[48,1536]{1,0:T(8,128)(2,1)}, u32[]{:S(2)}, u32[]{:S(2)}) collective-permute-start(bf16[48,1536]{1,0:T(8,128)(2,1)} %refs_0_), channel_id=1, source_target_pairs={{32,0},{33,1},{34,2},{35,3},{36,4},{37,5},{38,6},{39,7},{40,8},{41... | collective-permute-start | bytes 442376 | tf_op jit(solution)/shard_map/tokens/ppermute | solution.py:40
  5.0 9.7 %collective-permute-start.3 = (bf16[48,1536]{1,0:T(8,128)(2,1)}, bf16[48,1536]{1,0:T(8,128)(2,1)}, u32[]{:S(2)}, u32[]{:S(2)}) collective-permute-start(bf16[48,1536]{1,0:T(8,128)(2,1)} %refs_0_), channel_id=1, source_target_pairs={{64,0},{65,1},{66,2},{67,3},{68,4},{69,5},{70,6},{71,7},{72,8},{73... | collective-permute-start | bytes 442376 | tf_op jit(solution)/shard_map/project/ppermute | solution.py:40
  11.4 4.0 %collective-permute-start.4 = (bf16[48,1536]{1,0:T(8,128)(2,1)}, bf16[48,1536]{1,0:T(8,128)(2,1)S(1)}, u32[]{:S(2)}, u32[]{:S(2)}) collective-permute-start(bf16[48,1536]{1,0:T(8,128)(2,1)} %collective-permute-done.refs_1_), channel_id=1, source_target_pairs={{64,0},{65,1},{66,2},{67,3},{68,4},{69,5},{70,6},{71,7},{72,8},{73... | collective-permute-start | bytes 442376 | tf_op jit(solution)/shard_map/project/ppermute | solution.py:40
  14.3 1.6 %collective-permute-start.5 = (bf16[48,1536]{1,0:T(8,128)(2,1)}, bf16[48,1536]{1,0:T(8,128)(2,1)S(1)}, u32[]{:S(2)}, u32[]{:S(2)}) collective-permute-start(bf16[48,1536]{1,0:T(8,128)(2,1)} %collective-permute-done.1.refs_2_), channel_id=1, source_target_pairs={{64,0},{65,1},{66,2},{67,3},{68,4},{69,5},{70,6},{71,7},{72,8},{73... | collective-permute-start | bytes 442376 | tf_op jit(solution)/shard_map/project/ppermute | solution.py:40
  14.3 1.8 %collective-permute-start.6 = (bf16[48,1536]{1,0:T(8,128)(2,1)}, bf16[48,1536]{1,0:T(8,128)(2,1)S(1)}, u32[]{:S(2)}, u32[]{:S(2)}) collective-permute-start(bf16[48,1536]{1,0:T(8,128)(2,1)} %collective-permute-done.2.refs_3_), channel_id=1, source_target_pairs={{64,0},{65,1},{66,2},{67,3},{68,4},{69,5},{70,6},{71,7},{72,8},{73... | collective-permute-start | bytes 442376 | tf_op jit(solution)/shard_map/project/ppermute | solution.py:40
  18.4 11.8 %collective-permute-start.7 = (bf16[3,128,384]{2,1,0:T(8,128)(2,1)S(1)}, bf16[3,128,384]{2,1,0:T(8,128)(2,1)S(1)}, u32[]{:S(2)}, u32[]{:S(2)}) collective-permute-start(bf16[3,128,384]{2,1,0:T(8,128)(2,1)S(1)} %get-tuple-element.43.refs_4_), channel_id=1, source_target_pairs={{1,0},{2,1},{3,2},{4,3},{5,4},{6,5},{7,6},{0,7},{9,8},{10,9},{11,1... | collective-permute-start | bytes 884744 | tf_op jit(solution)/shard_map/exchange/ppermute | solution.py:40
  24.0 9.5 %collective-permute-start.11 = (bf16[3,128,384]{2,1,0:T(8,128)(2,1)S(1)}, bf16[3,128,384]{2,1,0:T(8,128)(2,1)S(1)}, u32[]{:S(2)}, u32[]{:S(2)}) collective-permute-start(bf16[3,128,384]{2,1,0:T(8,128)(2,1)S(1)} %get-tuple-element.43.refs_4_), channel_id=1, source_target_pairs={{7,0},{0,1},{1,2},{2,3},{3,4},{4,5},{5,6},{6,7},{15,8},{8,9},{9,10... | collective-permute-start | bytes 884744 | tf_op jit(solution)/shard_map/exchange/ppermute | solution.py:40
  24.0 9.5 %collective-permute-start.15 = (bf16[3,64,384]{2,1,0:T(8,128)(2,1)S(1)}, bf16[3,64,384]{2,1,0:T(8,128)(2,1)S(1)}, u32[]{:S(2)}, u32[]{:S(2)}) collective-permute-start(bf16[3,64,384]{2,1,0:T(8,128)(2,1)S(1)} %get-tuple-element.45.refs_0_), channel_id=1, source_target_pairs={{8,0},{9,1},{10,2},{11,3},{12,4},{13,5},{14,6},{15,7},{16,8},{17,9... | collective-permute-start | bytes 442376 | tf_op jit(solution)/shard_map/exchange/ppermute | solution.py:40
  26.8 7.3 %collective-permute-start.16 = (bf16[3,64,384]{2,1,0:T(8,128)(2,1)S(1)}, bf16[3,64,384]{2,1,0:T(8,128)(2,1)S(1)}, u32[]{:S(2)}, u32[]{:S(2)}) collective-permute-start(bf16[3,64,384]{2,1,0:T(8,128)(2,1)S(1)} %get-tuple-element.45.refs_0_), channel_id=1, source_target_pairs={{24,0},{25,1},{26,2},{27,3},{28,4},{29,5},{30,6},{31,7},{0,8},{1,9... | collective-permute-start | bytes 442376 | tf_op jit(solution)/shard_map/exchange/ppermute | solution.py:40
  26.8 7.8 %collective-permute-start.17 = (bf16[3,64,384]{2,1,0:T(8,128)(2,1)S(1)}, bf16[3,64,384]{2,1,0:T(8,128)(2,1)S(1)}, u32[]{:S(2)}, u32[]{:S(2)}) collective-permute-start(bf16[3,64,384]{2,1,0:T(8,128)(2,1)S(1)} %get-tuple-element.45.refs_0_), channel_id=1, source_target_pairs={{16,0},{17,1},{18,2},{19,3},{20,4},{21,5},{22,6},{23,7},{24,8},{25... | collective-permute-start | bytes 442376 | tf_op jit(solution)/shard_map/exchange/ppermute | solution.py:40
  30.1 27.5 %collective-permute-start.8 = (bf16[3,128,384]{2,1,0:T(8,128)(2,1)S(1)}, bf16[3,128,384]{2,1,0:T(8,128)(2,1)S(1)}, u32[]{:S(2)}, u32[]{:S(2)}) collective-permute-start(bf16[3,128,384]{2,1,0:T(8,128)(2,1)S(1)} %collective-permute-done.7.refs_5_), channel_id=1, source_target_pairs={{1,0},{2,1},{3,2},{4,3},{5,4},{6,5},{7,6},{0,7},{9,8},{10,9},{11,1... | collective-permute-start | bytes 884744 | tf_op jit(solution)/shard_map/exchange/ppermute | solution.py:40
  33.6 26.5 %collective-permute-start.12 = (bf16[3,128,384]{2,1,0:T(8,128)(2,1)S(1)}, bf16[3,128,384]{2,1,0:T(8,128)(2,1)S(1)}, u32[]{:S(2)}, u32[]{:S(2)}) collective-permute-start(bf16[3,128,384]{2,1,0:T(8,128)(2,1)S(1)} %collective-permute-done.11.refs_6_), channel_id=1, source_target_pairs={{7,0},{0,1},{1,2},{2,3},{3,4},{4,5},{5,6},{6,7},{15,8},{8,9},{9,10... | collective-permute-start | bytes 884744 | tf_op jit(solution)/shard_map/exchange/ppermute | solution.py:40
  57.6 23.4 %collective-permute-start.9 = (bf16[3,128,384]{2,1,0:T(8,128)(2,1)S(1)}, bf16[3,128,384]{2,1,0:T(8,128)(2,1)S(1)}, u32[]{:S(2)}, u32[]{:S(2)}) collective-permute-start(bf16[3,128,384]{2,1,0:T(8,128)(2,1)S(1)} %collective-permute-done.8.refs_0_), channel_id=1, source_target_pairs={{1,0},{2,1},{3,2},{4,3},{5,4},{6,5},{7,6},{0,7},{9,8},{10,9},{11,1... | collective-permute-start | bytes 884744 | tf_op jit(solution)/shard_map/exchange/ppermute | solution.py:40
  60.1 23.7 %collective-permute-start.13 = (bf16[3,128,384]{2,1,0:T(8,128)(2,1)S(1)}, bf16[3,128,384]{2,1,0:T(8,128)(2,1)S(1)}, u32[]{:S(2)}, u32[]{:S(2)}) collective-permute-start(bf16[3,128,384]{2,1,0:T(8,128)(2,1)S(1)} %collective-permute-done.12.refs_1_), channel_id=1, source_target_pairs={{7,0},{0,1},{1,2},{2,3},{3,4},{4,5},{5,6},{6,7},{15,8},{8,9},{9,10... | collective-permute-start | bytes 884744 | tf_op jit(solution)/shard_map/exchange/ppermute | solution.py:40
  81.0 19.8 %collective-permute-start.10 = (bf16[3,64,384]{2,1,0:T(8,128)(2,1)S(1)}, bf16[3,64,384]{2,1,0:T(8,128)(2,1)S(1)}, u32[]{:S(2)}, u32[]{:S(2)}) collective-permute-start(bf16[3,64,384]{2,1,0:T(8,128)(2,1)S(1)} %slice.8), channel_id=1, source_target_pairs={{1,0},{2,1},{3,2},{4,3},{5,4},{6,5},{7,6},{0,7},{9,8},{10,9},{11,1... | collective-permute-start | bytes 442376 | tf_op jit(solution)/shard_map/exchange/ppermute | solution.py:40
  83.8 17.0 %collective-permute-start.14 = (bf16[3,64,384]{2,1,0:T(8,128)(2,1)S(1)}, bf16[3,64,384]{2,1,0:T(8,128)(2,1)S(1)}, u32[]{:S(2)}, u32[]{:S(2)}) collective-permute-start(bf16[3,64,384]{2,1,0:T(8,128)(2,1)S(1)} %slice.9), channel_id=1, source_target_pairs={{7,0},{0,1},{1,2},{2,3},{3,4},{4,5},{5,6},{6,7},{15,8},{8,9},{9,10... | collective-permute-start | bytes 442376 | tf_op jit(solution)/shard_map/exchange/ppermute | solution.py:40
  115.4 5.5 %collective-permute-start.18 = (bf16[224,384]{1,0:T(8,128)(2,1)S(1)}, bf16[224,384]{1,0:T(8,128)(2,1)S(1)}, u32[]{:S(2)}, u32[]{:S(2)}) collective-permute-start(bf16[224,384]{1,0:T(8,128)(2,1)S(1)} %get-tuple-element.60), channel_id=1, source_target_pairs={{24,0},{25,1},{26,2},{27,3},{28,4},{29,5},{30,6},{31,7},{0,8},{1,9... | collective-permute-start | bytes 516104 | tf_op jit(solution)/shard_map/combine/ppermute | solution.py:40
  116.0 6.3 %collective-permute-start.19 = (bf16[224,384]{1,0:T(8,128)(2,1)S(1)}, bf16[224,384]{1,0:T(8,128)(2,1)S(1)}, u32[]{:S(2)}, u32[]{:S(2)}) collective-permute-start(bf16[224,384]{1,0:T(8,128)(2,1)S(1)} %get-tuple-element.61), channel_id=1, source_target_pairs={{8,0},{9,1},{10,2},{11,3},{12,4},{13,5},{14,6},{15,7},{16,8},{17,9... | collective-permute-start | bytes 516104 | tf_op jit(solution)/shard_map/combine/ppermute | solution.py:40
  118.2 7.2 %collective-permute-start.20 = (bf16[224,384]{1,0:T(8,128)(2,1)S(1)}, bf16[224,384]{1,0:T(8,128)(2,1)S(1)}, u32[]{:S(2)}, u32[]{:S(2)}) collective-permute-start(bf16[224,384]{1,0:T(8,128)(2,1)S(1)} %get-tuple-element.62), channel_id=1, source_target_pairs={{16,0},{17,1},{18,2},{19,3},{20,4},{21,5},{22,6},{23,7},{24,8},{25... | collective-permute-start | bytes 516104 | tf_op jit(solution)/shard_map/combine/ppermute | solution.py:40
  125.6 5.1 %collective-permute-start.21 = (bf16[192,192]{1,0:T(8,128)(2,1)S(1)}, bf16[192,192]{1,0:T(8,128)(2,1)S(1)}, u32[]{:S(2)}, u32[]{:S(2)}) collective-permute-start(bf16[192,192]{1,0:T(8,128)(2,1)S(1)} %get-tuple-element.63), channel_id=1, source_target_pairs={{32,0},{33,1},{34,2},{35,3},{36,4},{37,5},{38,6},{39,7},{40,8},{41... | collective-permute-start | bytes 221192 | tf_op jit(solution)/shard_map/output/ppermute | solution.py:40
  131.0 6.6 %collective-permute-start.22 = (bf16[96,1536]{1,0:T(8,128)(2,1)S(1)}, bf16[96,1536]{1,0:T(8,128)(2,1)S(1)}, u32[]{:S(2)}, u32[]{:S(2)}) collective-permute-start(bf16[96,1536]{1,0:T(8,128)(2,1)S(1)} %get-tuple-element.68), channel_id=1, source_target_pairs={{64,0},{65,1},{66,2},{67,3},{68,4},{69,5},{70,6},{71,7},{72,8},{73... | collective-permute-start | bytes 884744 | tf_op jit(solution)/shard_map/output/ppermute | solution.py:40
  137.7 5.1 %collective-permute-start.23 = (bf16[48,1536]{1,0:T(8,128)(2,1)S(1)}, bf16[48,1536]{1,0:T(8,128)(2,1)S(1)}, u32[]{:S(2)}, u32[]{:S(2)}) collective-permute-start(bf16[48,1536]{1,0:T(8,128)(2,1)S(1)} %get-tuple-element.70), channel_id=1, source_target_pairs={{0,128},{1,129},{2,130},{3,131},{4,132},{5,133},{6,134},{7,135},{8... | collective-permute-start | bytes 442376 | tf_op jit(solution)/shard_map/output/ppermute | solution.py:47
  (8 other events, 76.3 us)
where the time goes:
time: 144 us
  Pallas kernels  79.3 us (55%)
  starting transfers between devices  38.3 us (27%)
  waiting for transfers between devices  22.4 us (16%)
  local copies, waits for them, and re-layouts  3.32 us (2%)
    pallas_call x13, Pallas kernels, call(): pl.pallas_call(kernel, out_shape=out_shape, in_specs=[scalar_spec] * len(...  79.3 us
    ppermute x23, starting transfers between devices, fetch(): return lax.ppermute(array, AXES, pairs)  38.2 us
    ppermute x23, waiting for transfers between devices, fetch(): return lax.ppermute(array, AXES, pairs)  17.3 us
    ppermute x1, waiting for transfers between devices, fetch_x_low(): return lax.ppermute(array, AXES, pairs)  5.02 us
    unnamed x18, local copies, waits for them, and re-layouts  3.28 us
  transfers between devices with their start and end apart: 24, of which 14 were waited for; matrix products, arithmetic and copies ran while one was open for 2% of the time, Pallas kernels for 43%

commit v1 on v0

v1 whole, which is shorter than its diff:
```python
import functools

import jax
import jax.numpy as jnp
from jax import lax
from jax.experimental import pallas as pl
from jax.experimental.pallas import tpu as pltpu
from jax.sharding import PartitionSpec as P

HEAD_DIM = 64
AXES = ("uly", "blk")
X, CORE, Y, Z = 4, 2, 4, 8
ONES = 16
VMEM_BYTES = 16 << 20
STATS = 16
LOG2_SCALE = 1.4426950408889634 * HEAD_DIM**-0.5
SAFE_SQUARE = 96.0**2
MASKED = -1e30
BF16, F32 = jnp.bfloat16, jnp.float32


def device_id(x, core, y, z):
    return ((x % 2) * CORE + core) * (2 * Y * Z) + (x // 2) * (Y * Z) + y * Z + z


def places():
    return [
        (x, core, y, z) for x in range(X) for core in range(CORE) for y in range(Y) for z in range(Z)
    ]


def fetch(array, dx=0, dcore=0, dy=0, dz=0):
    pairs = [
        (
            device_id((x + dx) % X, (core + dcore) % CORE, (y + dy) % Y, (z + dz) % Z),
            device_id(x, core, y, z),
        )
        for x, core, y, z in places()
    ]
    return lax.ppermute(array, AXES, pairs)


def fetch_x_low(array):
    pairs = [
        (device_id(x, core, y, z), device_id(x ^ 1, core, y, z)) for x, core, y, z in places()
    ]
    return lax.ppermute(array, AXES, pairs)


def call(kernel, out_shape, flops, *operands, exps=0, aliases=None, scratch=(), scalars=(), name=None):
    spec = pl.BlockSpec(memory_space=pltpu.VMEM)
    scalar_spec = pl.BlockSpec(memory_space=pltpu.SMEM)
    moved = sum(a.size * a.dtype.itemsize for a in operands)
    return pl.pallas_call(
        kernel,
        out_shape=out_shape,
        in_specs=[scalar_spec] * len(scalars) + [spec] * len(operands),
        out_specs=jax.tree.map(lambda _: spec, out_shape),
        input_output_aliases=aliases or {},
        scratch_shapes=scratch,
        compiler_params=pltpu.CompilerParams(vmem_limit_bytes=VMEM_BYTES),
        cost_estimate=pl.CostEstimate(flops=flops, bytes_accessed=moved, transcendentals=exps),
        name=name,
    )(*scalars, *operands)


def shape(dims, dtype):
    return jax.ShapeDtypeStruct(dims, dtype)


def halves_kernel(width, high_ref, *refs):
    parts, out_ref = refs[:-1], refs[-1]
    at = 0
    for part in parts:
        for cut in range(0, part.shape[1], 2 * width):
            low, high = part[:, cut : cut + width], part[:, cut + width : cut + 2 * width]
            out_ref[:, at : at + width] = jnp.where(high_ref[0] == 1, high, low)
            at += width


def half_row(high_ref, bias_ref, row_ref):
    width = bias_ref.shape[1] // 2
    for at in range(bias_ref.shape[0]):
        low, high = bias_ref[at : at + 1, :width], bias_ref[at : at + 1, width:]
        row_ref[0:1, at * width : (at + 1) * width] = jnp.where(high_ref[0] == 1, high, low)
    return row_ref[0:1, :]


def project_kernel(high_ref, w_ref, bias_ref, *refs):
    blocks, (q_ref, kv_ref, tokens, row_ref) = refs[:-4], refs[-4:]
    heads = q_ref.shape[0]
    width = heads * HEAD_DIM
    rows = blocks[0].shape[0]
    for at, block in enumerate(blocks):
        tokens[at * rows : (at + 1) * rows, :] = block[...]
    projected = jnp.dot(tokens[...], w_ref[...], preferred_element_type=F32)
    projected = projected + half_row(high_ref, bias_ref, row_ref)
    columns = projected.T.astype(BF16)
    for h in range(heads):
        cut = h * HEAD_DIM
        q_ref[h] = columns[cut : cut + HEAD_DIM]
        kv_ref[h, :HEAD_DIM, :] = columns[width + cut : width + cut + HEAD_DIM]
        kv_ref[h, HEAD_DIM:, :] = columns[2 * width + cut : 2 * width + cut + HEAD_DIM]


def text_kernel(high_ref, text_ref, w_ref, bias_ref, kv_ref, rows_ref, row_ref):
    heads = kv_ref.shape[0]
    width = heads * HEAD_DIM
    count = text_ref.shape[0]
    rows_ref[...] = jnp.zeros_like(rows_ref)
    rows = jnp.dot(text_ref[...], w_ref[...], preferred_element_type=F32)
    rows_ref[:count, :] = rows + half_row(high_ref, bias_ref, row_ref)
    columns = rows_ref[...].T.astype(BF16)
    for h in range(heads):
        cut = h * HEAD_DIM
        kv_ref[h, :HEAD_DIM, :] = columns[cut : cut + HEAD_DIM]
        kv_ref[h, HEAD_DIM:, :] = columns[width + cut : width + cut + HEAD_DIM]


def scale_queries(parts, q2_ref, norm_ref):
    for h in range(q2_ref.shape[0]):
        largest = None
        for at, part in enumerate(parts):
            scaled = part[h].astype(F32) * LOG2_SCALE
            high = scaled.astype(BF16)
            low = (scaled - high.astype(F32)).astype(BF16)
            here = slice(at * part.shape[2], (at + 1) * part.shape[2])
            q2_ref[h, :HEAD_DIM, here] = high
            q2_ref[h, HEAD_DIM:, here] = low
            top = jnp.max(jnp.sum(scaled * scaled, axis=0, keepdims=True), axis=1, keepdims=True)
            largest = top if largest is None else jnp.maximum(largest, top)
        norm_ref[h] = jnp.broadcast_to(largest, norm_ref.shape[1:])


def keys_of(parts, h):
    return jnp.concatenate([k[h, :HEAD_DIM, :] for k, _ in parts], axis=1)


def values_of(parts, h, count):
    values = jnp.concatenate([v[h, -HEAD_DIM:, :] for _, v in parts], axis=1)
    ones = jnp.ones((ONES, values.shape[1]), BF16)
    if count is not None:
        inside = lax.broadcasted_iota(jnp.int32, ones.shape, 1) < count
        ones = jnp.where(inside, 1.0, 0.0).astype(BF16)
    return jnp.concatenate([values, ones], axis=0)


def attend(parts, q2_ref, norm_ref, bound, state_in, acc_ref, m_ref, bound_ref, tile, count=None):
    heads, _, queries = acc_ref.shape
    worst = None
    for h in range(heads):
        keys = keys_of(parts, h).astype(F32)
        top = jnp.max(jnp.sum(keys * keys, axis=0, keepdims=True), axis=1, keepdims=True)
        product = top * norm_ref[h, 0:1, 0:1]
        worst = product if worst is None else jnp.maximum(worst, product)
    if bound is not None:
        worst = jnp.maximum(worst, bound[0:1, 0:1])
    bound_ref[...] = jnp.broadcast_to(worst, bound_ref.shape)
    safe = jnp.max(worst) <= SAFE_SQUARE

    def doubled_keys(h):
        keys = keys_of(parts, h)
        return jnp.concatenate([keys, keys], axis=0).T

    @pl.when(safe)
    def _():
        def one_head(h, carry):
            keys, values = doubled_keys(h), values_of(parts, h, count)
            for at in range(0, queries, tile):
                here = slice(at, at + tile)
                scores = jnp.dot(keys, q2_ref[h, :, here], preferred_element_type=F32)
                weights = jnp.exp2(scores).astype(BF16)
                term = jnp.dot(values, weights, preferred_element_type=F32)
                acc_ref[h, :, here] = term if state_in is None else state_in[0][h, :, here] + term
            return carry

        lax.fori_loop(0, heads, one_head, 0)
        m_ref[...] = jnp.zeros_like(m_ref) if state_in is None else state_in[1][...]

    @pl.when(jnp.logical_not(safe))
    def _():
        step = 128

        def one_head(h, carry):
            keys, values = doubled_keys(h), values_of(parts, h, count)

            def one_tile(at, carry):
                here = pl.ds(pl.multiple_of(at * step, step), step)
                scores = jnp.dot(keys, q2_ref[h, :, here], preferred_element_type=F32)
                if count is not None:
                    inside = lax.broadcasted_iota(jnp.int32, scores.shape, 0) < count
                    scores = jnp.where(inside, scores, MASKED)
                top = jnp.max(scores, axis=0, keepdims=True)
                if state_in is not None:
                    before = state_in[1][h, 0:1, here]
                    top = jnp.maximum(top, before)
                weights = jnp.exp2(scores - top).astype(BF16)
                term = jnp.dot(values, weights, preferred_element_type=F32)
                if state_in is not None:
                    term = term + state_in[0][h, :, here] * jnp.exp2(before - top)
                acc_ref[h, :, here] = term
                m_ref[h, :, here] = jnp.broadcast_to(top, (m_ref.shape[1], step))
                return carry

            return lax.fori_loop(0, queries // step, one_tile, carry)

        lax.fori_loop(0, heads, one_head, 0)


def first_kernel(n_parts, tile, *refs):
    q_refs, kv_refs = refs[:Y], refs[Y : Y + n_parts]
    acc_ref, m_ref, bound_ref, q2_ref, norm_ref = refs[Y + n_parts :]
    scale_queries(q_refs, q2_ref, norm_ref)
    parts = [(r, r) for r in kv_refs]
    attend(parts, q2_ref, norm_ref, None, None, acc_ref, m_ref, bound_ref, tile)


def next_kernel(n_parts, tile, count, *refs):
    kv_refs, refs = refs[:n_parts], refs[n_parts:]
    q2_ref, norm_ref, acc_in, m_in, bound_in, acc_ref, m_ref, bound_ref = refs
    parts = [(r, r) for r in kv_refs]
    state = (acc_in, m_in)
    attend(parts, q2_ref, norm_ref, bound_in, state, acc_ref, m_ref, bound_ref, tile, count)


def in_parts(value, count):
    parts = []
    for _ in range(count):
        parts.append(value.astype(BF16).astype(F32))
        value = value - parts[-1]
    return parts


def last_kernel(tile, k_ref, v_ref, *refs):
    q2_ref, norm_ref, acc_in, m_in, bound_in, own_acc, own_m, bound_ref = refs[:8]
    packs, (acc_ref, m_ref) = refs[8:-2], refs[-2:]
    parts = [(k_ref, v_ref)]
    state = (acc_in, m_in)
    attend(parts, q2_ref, norm_ref, bound_in, state, acc_ref, m_ref, bound_ref, tile)
    heads, _, queries = q2_ref.shape
    mine = queries // Y
    own_acc[...] = acc_ref[:, :, :mine]
    own_m[...] = m_ref[:, :, :mine]
    for at, pack in enumerate(packs):
        here = slice((at + 1) * mine, (at + 2) * mine)
        rows = []
        for h in range(heads):
            pack[h * HEAD_DIM : (h + 1) * HEAD_DIM, :] = acc_ref[h, :HEAD_DIM, here].astype(BF16)
            rows += in_parts(acc_ref[h, HEAD_DIM : HEAD_DIM + 1, here], 2)
            rows += in_parts(m_ref[h, 0:1, here], 3)
        rows.append(jnp.zeros((STATS - len(rows), mine), F32))
        pack[heads * HEAD_DIM :, :] = jnp.concatenate(rows, axis=0).astype(BF16)


def combine_kernel(acc_ref, m_ref, *refs):
    packs, pieces = refs[:-X], refs[-X:]
    heads, _, mine = acc_ref.shape
    columns = []
    for h in range(heads):
        sums = [acc_ref[h, :HEAD_DIM, :]]
        totals = [acc_ref[h, HEAD_DIM : HEAD_DIM + 1, :]]
        tops = [m_ref[h, 0:1, :]]
        for pack in packs:
            sums.append(pack[h * HEAD_DIM : (h + 1) * HEAD_DIM, :].astype(F32))
            stats = pack[heads * HEAD_DIM :, :].astype(F32)
            at = 5 * h
            totals.append(stats[at : at + 1] + stats[at + 1 : at + 2])
            tops.append(stats[at + 2 : at + 3] + stats[at + 3 : at + 4] + stats[at + 4 : at + 5])
        top = functools.reduce(jnp.maximum, tops)
        shares = [jnp.exp2(t - top) for t in tops]
        total = sum(t * s for t, s in zip(totals, shares))
        mixed = sum(a * s for a, s in zip(sums, shares))
        columns.append(mixed / total)
    rows = jnp.concatenate(columns, axis=0).T.astype(BF16)
    block = mine // (X * CORE)
    for core in range(CORE):
        for at, piece in enumerate(pieces):
            start = (core * X + at) * block
            piece[core * block : (core + 1) * block, :] = rows[start : start + block]


def out_rows(piece, w_ref, half):
    width = piece.shape[1]
    here = pl.ds(pl.multiple_of(half * width, width), width)
    return jnp.dot(piece[...], w_ref[here, :], preferred_element_type=F32)


def near_kernel(high_ref, piece, w_ref, out_ref):
    out_ref[...] = out_rows(piece, w_ref, high_ref[0])


def far_kernel(high_ref, near_ref, up, down, across, w_ref, w_side_ref, kept_ref, sent_ref):
    total = near_ref[...] + out_rows(across, w_ref, high_ref[2])
    total = total + out_rows(up, w_side_ref, high_ref[0]) + out_rows(down, w_side_ref, high_ref[1])
    half = kept_ref.shape[0]
    kept_ref[...] = total[:half]
    sent_ref[...] = total[half:].astype(BF16)


def finish_kernel(kept_ref, received_ref, bias_ref, out_ref):
    out_ref[...] = (kept_ref[...] + received_ref[...].astype(F32) + bias_ref[...]).astype(BF16)


def body(
    image_tokens, text_tokens, w_query_key, w_value, qkv_bias, w_text, text_bias, w_out, out_bias
):
    block, model_width = image_tokens.shape
    local_width = w_value.shape[1]
    width = local_width // 2
    heads = width // HEAD_DIM
    mine = block * X * CORE
    queries = mine * Y
    text_count = text_tokens.shape[0]
    text_rows = -(-text_count // 128) * 128
    blk, uly = lax.axis_index("blk"), lax.axis_index("uly")
    x_high = blk // (Y * Z)
    x_at, core_at = x_high * 2 + uly // CORE, uly % CORE

    with jax.named_scope("tokens"):
        near = [image_tokens] + [fetch(image_tokens, dx=d) for d in (1, -1, 2)]

    with jax.named_scope("weights"):
        high = x_high.reshape(1).astype(jnp.int32)

        def halves(*parts):
            columns = sum(p.shape[1] for p in parts) // 2
            return call(
                functools.partial(halves_kernel, width),
                shape((model_width, columns), BF16),
                0,
                *parts,
                scalars=(high,),
                name="halves",
            )

        weights = halves(w_query_key.reshape(model_width, 2 * local_width), w_value)

    with jax.named_scope("project"):
        sibling = fetch(image_tokens, dcore=1)
        near, weights = lax.optimization_barrier((near, weights))
        blocks = near + [sibling] + [fetch(block_rows, dcore=1) for block_rows in near[1:]]
        q_own, kv_own = call(
            project_kernel,
            (shape((heads, HEAD_DIM, mine), BF16), shape((heads, 2 * HEAD_DIM, mine), BF16)),
            6 * mine * model_width * width,
            weights,
            qkv_bias,
            *blocks,
            scalars=(high,),
            scratch=[pltpu.VMEM((mine, model_width), BF16), pltpu.VMEM((8, 3 * width), F32)],
            name="project",
        )
    with jax.named_scope("exchange"):
        up = [fetch(kv_own, dz=1)]
        down = [fetch(kv_own, dz=-1)]
        q_parts = [q_own] + [fetch(q_own, dy=d) for d in (1, -1, 2)]
        for _ in range(2):
            up.append(fetch(up[-1], dz=1))
            down.append(fetch(down[-1], dz=-1))
        w_from, up[1] = lax.optimization_barrier((w_out, up[1]))
        w_side = fetch_x_low(w_from)
        far_keys = fetch(up[-1][:, :HEAD_DIM], dz=1)
        far_values = fetch(down[-1][:, HEAD_DIM:], dz=-1)

    def state_shapes(count):
        return (
            shape((heads, HEAD_DIM + ONES, count), F32),
            shape((heads, 8, count), F32),
            shape((8, 128), F32),
        )

    def query_shapes(count):
        return (shape((heads, 2 * HEAD_DIM, count), BF16), shape((heads, 8, 128), F32))

    def costs(rows, columns):
        return 2500 * heads * rows * columns

    with jax.named_scope("attend"):
        acc, m, bound, q2, norm = call(
            functools.partial(first_kernel, 3, 768),
            state_shapes(queries) + query_shapes(queries),
            costs(queries, 3 * mine),
            *q_parts,
            kv_own,
            up[0],
            down[0],
            exps=0,
            name="attend_first",
        )
        for at in (1, 2):
            acc, m, bound = call(
                functools.partial(next_kernel, 2, 768, None),
                state_shapes(queries),
                costs(queries, 2 * mine),
                up[at],
                down[at],
                q2,
                norm,
                acc,
                m,
                bound,
                exps=0,
                aliases={n + 4: n for n in range(3)},
                name="attend_next",
            )
        pack = shape((heads * HEAD_DIM + STATS, mine), BF16)
        acc, m, bound, *packs = call(
            functools.partial(last_kernel, 1536),
            state_shapes(mine) + (pack,) * (Y - 1),
            costs(queries, mine),
            far_keys,
            far_values,
            q2,
            norm,
            acc,
            m,
            bound,
            exps=0,
            scratch=[pltpu.VMEM(s.shape, s.dtype) for s in state_shapes(queries)[:2]],
            name="attend_last",
        )

    with jax.named_scope("text"):
        packs, w_text, q2, acc = lax.optimization_barrier((packs, w_text, q2, acc))
        text_kv = call(
            text_kernel,
            shape((heads, 2 * HEAD_DIM, text_rows), BF16),
            4 * text_rows * model_width * width,
            text_tokens,
            halves(w_text.reshape(model_width, 2 * local_width)),
            text_bias,
            scalars=(high,),
            scratch=[pltpu.VMEM((text_rows, 2 * width), F32), pltpu.VMEM((8, 2 * width), F32)],
            name="text_project",
        )
        acc, m, _ = call(
            functools.partial(next_kernel, 1, mine, text_count),
            state_shapes(mine),
            costs(mine, text_rows),
            text_kv,
            q2,
            norm,
            acc,
            m,
            bound,
            aliases={n + 3: n for n in range(3)},
            name="attend_text",
        )

    with jax.named_scope("combine"):
        returned = [fetch(pack, dy=-d) for pack, d in zip(packs, (1, -1, 2))]
        piece = shape((CORE * block, width), BF16)
        pieces = call(combine_kernel, (piece,) * X, 0, acc, m, *returned, name="combine")

    with jax.named_scope("output"):
        distances = (1, -1, 2)
        received = [fetch(p, dx=-d) for p, d in zip(pieces[1:], distances)]
        flops = 2 * CORE * block * width * model_width
        total = call(
            near_kernel,
            shape((CORE * block, model_width), F32),
            flops,
            pieces[0],
            w_out,
            scalars=(high,),
            name="output_near",
        )
        received, total = lax.optimization_barrier((received, total))
        highs = jnp.stack([lax.rem(x_at - d + X, X) // 2 for d in distances]).astype(jnp.int32)
        kept, sent = call(
            far_kernel,
            (shape((block, model_width), F32), shape((block, model_width), BF16)),
            3 * flops,
            total,
            *received,
            w_out,
            w_side,
            scalars=(highs,),
            name="output_far",
        )
        return call(
            finish_kernel,
            shape((block, model_width), BF16),
            0,
            kept,
            fetch(sent, dcore=1),
            out_bias.reshape(1, -1),
            name="finish",
        )


def solution(mesh):
    in_specs = (
        P(("uly", "blk"), None),
        P(),
        P(None, None, "uly"),
        P(None, "uly"),
        P(None, "uly"),
        P(None, None, "uly"),
        P(None, "uly"),
        P("uly", None),
        P(),
    )
    out_specs = P(("uly", "blk"), None)
    return jax.shard_map(body, mesh=mesh, in_specs=in_specs, out_specs=out_specs, check_vma=False)
```

time: 144 us -> 138 us (0.958)
  waiting for transfers between devices: 22.4 us -> 10.4 us
  starting transfers between devices: 38.3 us -> 40.8 us
  local copies, waits for them, and re-layouts: 3.32 us -> 5.41 us
    ppermute x23 -> x25, waiting for transfers between devices: 17.3 us -> 10.4 us  [fetch(): return lax.ppermute(array, AXES, pairs)]
    ppermute x1, waiting for transfers between devices: 5.02 us -> 0.01 us  [fetch_x_low(): return lax.ppermute(array, AXES, pairs)]
    ppermute x23 -> x25, starting transfers between devices: 38.2 us -> 40.7 us  [fetch(): return lax.ppermute(array, AXES, pairs)]
    unnamed x18 -> x20, local copies, waits for them, and re-layouts: 3.28 us -> 5.37 us
  transfers between devices with their start and end apart: 24 -> 26, of which waited for: 14 -> 12; matrix products, arithmetic and copies ran while one was open for 2% -> 3% of each run, Pallas kernels for 43% -> 56%
where the time goes in v1:
time: 138 us; the launch traced here: 137 us
  Pallas kernels  80.4 us (58%)
  starting transfers between devices  40.8 us (30%)
  waiting for transfers between devices  10.4 us (8%)
  local copies, waits for them, and re-layouts  5.41 us (4%)
    pallas_call x13, Pallas kernels, call(): pl.pallas_call(kernel, out_shape=out_shape, in_specs=[scalar_spec] * len(...  80.4 us
    ppermute x25, starting transfers between devices, fetch(): return lax.ppermute(array, AXES, pairs)  40.7 us
    ppermute x25, waiting for transfers between devices, fetch(): return lax.ppermute(array, AXES, pairs)  10.4 us
    unnamed x20, local copies, waits for them, and re-layouts  5.37 us
  transfers between devices with their start and end apart: 26, of which 12 were waited for; matrix products, arithmetic and copies ran while one was open for 3% of the time, Pallas kernels for 56%

profile of v1, /device:TPU:1, one launch (start us, length us, event | category | flops | bytes accessed | tf_op | source)
XLA Modules:
  0.0 137.3 jit_solution(11039775908357183704)
XLA Ops:
  0.0 3.3 %collective-permute-start = (bf16[48,1536]{1,0:T(8,128)(2,1)}, bf16[48,1536]{1,0:T(8,128)(2,1)}, u32[]{:S(2)}, u32[]{:S(2)}) collective-permute-start(bf16[48,1536]{1,0:T(8,128)(2,1)} %refs_0_), channel_id=1, source_target_pairs={{128,0},{129,1},{130,2},{131,3},{132,4},{133,5},{134,6},{135,7},{1... | collective-permute-start | bytes 442376 | tf_op jit(solution)/shard_map/tokens/ppermute | solution.py:40
  3.3 1.7 %collective-permute-start.2 = (bf16[48,1536]{1,0:T(8,128)(2,1)}, bf16[48,1536]{1,0:T(8,128)(2,1)}, u32[]{:S(2)}, u32[]{:S(2)}) collective-permute-start(bf16[48,1536]{1,0:T(8,128)(2,1)} %refs_0_), channel_id=1, source_target_pairs={{32,0},{33,1},{34,2},{35,3},{36,4},{37,5},{38,6},{39,7},{40,8},{41... | collective-permute-start | bytes 442376 | tf_op jit(solution)/shard_map/tokens/ppermute | solution.py:40
  5.0 1.5 %collective-permute-start.3 = (bf16[48,1536]{1,0:T(8,128)(2,1)}, bf16[48,1536]{1,0:T(8,128)(2,1)}, u32[]{:S(2)}, u32[]{:S(2)}) collective-permute-start(bf16[48,1536]{1,0:T(8,128)(2,1)} %refs_0_), channel_id=1, source_target_pairs={{64,0},{65,1},{66,2},{67,3},{68,4},{69,5},{70,6},{71,7},{72,8},{73... | collective-permute-start | bytes 442376 | tf_op jit(solution)/shard_map/project/ppermute | solution.py:40
  6.6 2.2 %copy.19 = bf16[192,8,2,384]{3,1,2,0:T(8,128)(2,1)S(1)} copy(bf16[192,8,2,384]{3,2,1,0:T(2,128)(2,1)} %bitcast.10) | data formatting | bytes 4718592
  11.4 2.8 %collective-permute-start.4 = (bf16[48,1536]{1,0:T(8,128)(2,1)}, bf16[48,1536]{1,0:T(8,128)(2,1)S(1)}, u32[]{:S(2)}, u32[]{:S(2)}) collective-permute-start(bf16[48,1536]{1,0:T(8,128)(2,1)} %collective-permute-done.refs_1_), channel_id=1, source_target_pairs={{64,0},{65,1},{66,2},{67,3},{68,4},{69,5},{70,6},{71,7},{72,8},{73... | collective-permute-start | bytes 442376 | tf_op jit(solution)/shard_map/project/ppermute | solution.py:40
  16.1 2.3 %project.1 = (bf16[3,64,384]{2,1,0:T(8,128)(2,1)S(1)}, bf16[3,128,384]{2,1,0:T(8,128)(2,1)S(1)}) custom-call(s32[1]{0:T(128)} %bitcast.3.high_ref, bf16[1536,576]{1,0:T(8,128)(2,1)S(1)} %halves.2.w_ref, f32[3,384]{1,0:T(4,128)S(1)} %copy-done.4, bf16[48,1536]{1,0:T(8,128)(2,1)S(1)} %copy-done.3, bf16[48,1536]{1,0:T(8,128)(2,1)} %collective-permute-done.refs_1_, ...), custom_call_target="tpu_custom_call" | custom-call | flops 679477248 | bytes 2953728 | tf_op jit(solution)/shard_map/project/project/pallas_call | solution.py:54
  18.4 5.7 %collective-permute-start.7 = (bf16[3,128,384]{2,1,0:T(8,128)(2,1)S(1)}, bf16[3,128,384]{2,1,0:T(8,128)(2,1)S(1)}, u32[]{:S(2)}, u32[]{:S(2)}) collective-permute-start(bf16[3,128,384]{2,1,0:T(8,128)(2,1)S(1)} %get-tuple-element.54.refs_4_), channel_id=1, source_target_pairs={{1,0},{2,1},{3,2},{4,3},{5,4},{6,5},{7,6},{0,7},{9,8},{10,9},{11,1... | collective-permute-start | bytes 884744 | tf_op jit(solution)/shard_map/exchange/ppermute | solution.py:40
  24.0 2.7 %collective-permute-start.15 = (bf16[3,64,384]{2,1,0:T(8,128)(2,1)S(1)}, bf16[3,64,384]{2,1,0:T(8,128)(2,1)S(1)}, u32[]{:S(2)}, u32[]{:S(2)}) collective-permute-start(bf16[3,64,384]{2,1,0:T(8,128)(2,1)S(1)} %get-tuple-element.55.refs_0_), channel_id=1, source_target_pairs={{8,0},{9,1},{10,2},{11,3},{12,4},{13,5},{14,6},{15,7},{16,8},{17,9... | collective-permute-start | bytes 442376 | tf_op jit(solution)/shard_map/exchange/ppermute | solution.py:40
  26.8 1.6 %collective-permute-start.17 = (bf16[3,64,384]{2,1,0:T(8,128)(2,1)S(1)}, bf16[3,64,384]{2,1,0:T(8,128)(2,1)S(1)}, u32[]{:S(2)}, u32[]{:S(2)}) collective-permute-start(bf16[3,64,384]{2,1,0:T(8,128)(2,1)S(1)} %get-tuple-element.55.refs_0_), channel_id=1, source_target_pairs={{16,0},{17,1},{18,2},{19,3},{20,4},{21,5},{22,6},{23,7},{24,8},{25... | collective-permute-start | bytes 442376 | tf_op jit(solution)/shard_map/exchange/ppermute | solution.py:40
  28.4 1.7 %collective-permute-done.7.refs_5_ = bf16[3,128,384]{2,1,0:T(8,128)(2,1)S(1)} collective-permute-done((bf16[3,128,384]{2,1,0:T(8,128)(2,1)S(1)}, bf16[3,128,384]{2,1,0:T(8,128)(2,1)S(1)}, u32[]{:S(2)}, u32[]{:S(2)}) %collective-permute-start.7) | collective-permute-done | bytes 294944 | tf_op jit(solution)/shard_map/exchange/ppermute | solution.py:40
  30.2 3.4 %collective-permute-start.8 = (bf16[3,128,384]{2,1,0:T(8,128)(2,1)S(1)}, bf16[3,128,384]{2,1,0:T(8,128)(2,1)S(1)}, u32[]{:S(2)}, u32[]{:S(2)}) collective-permute-start(bf16[3,128,384]{2,1,0:T(8,128)(2,1)S(1)} %collective-permute-done.7.refs_5_), channel_id=1, source_target_pairs={{1,0},{2,1},{3,2},{4,3},{5,4},{6,5},{7,6},{0,7},{9,8},{10,9},{11,1... | collective-permute-start | bytes 884744 | tf_op jit(solution)/shard_map/exchange/ppermute | solution.py:40
  34.6 20.5 %attend_first.1 = (f32[3,80,1536]{2,1,0:T(8,128)S(1)}, f32[3,8,1536]{2,1,0:T(8,128)S(1)}, f32[8,128]{1,0:T(8,128)S(1)}, bf16[3,128,1536]{2,1,0:T(8,128)(2,1)S(1)}, f32[3,8,128]{2,1,0:T(8,128)S(1)}) custom-call(bf16[3,64,384]{2,1,0:T(8,128)(2,1)S(1)} %get-tuple-element.55.refs_0_, bf16[3,64,384]{2,1,0:T(8,128)(2,1)S(1)} %collective-permute-done.15.refs_1_, ...), custom_call_target="tpu_custom_call" | custom-call | flops 13271040000 | bytes 1474560 | tf_op jit(solution)/shard_map/attend/attend_first/pallas_call | solution.py:54
  55.2 2.5 %collective-permute-start.9 = (bf16[3,128,384]{2,1,0:T(8,128)(2,1)S(1)}, bf16[3,128,384]{2,1,0:T(8,128)(2,1)S(1)}, u32[]{:S(2)}, u32[]{:S(2)}) collective-permute-start(bf16[3,128,384]{2,1,0:T(8,128)(2,1)S(1)} %collective-permute-done.8.refs_0_), channel_id=1, source_target_pairs={{1,0},{2,1},{3,2},{4,3},{5,4},{6,5},{7,6},{0,7},{9,8},{10,9},{11,1... | collective-permute-start | bytes 884744 | tf_op jit(solution)/shard_map/exchange/ppermute | solution.py:40
  57.7 16.9 %attend_next.2 = (f32[3,80,1536]{2,1,0:T(8,128)S(1)}, f32[3,8,1536]{2,1,0:T(8,128)S(1)}, f32[8,128]{1,0:T(8,128)S(1)}) custom-call(bf16[3,128,384]{2,1,0:T(8,128)(2,1)S(1)} %collective-permute-done.8.refs_0_, bf16[3,128,384]{2,1,0:T(8,128)(2,1)S(1)} %collective-permute-done.12.refs_1_, ...), custom_call_target="tpu_custom_call", output_to_operand_aliasing={{0}: (4, {}), {1}: (5, {}), {2}: (6, {})} | custom-call | flops 8847360000 | bytes 3407872 | tf_op jit(solution)/shard_map/attend/attend_next/pallas_call | solution.py:54
  74.7 2.7 %collective-permute-start.10 = (bf16[3,64,384]{2,1,0:T(8,128)(2,1)S(1)}, bf16[3,64,384]{2,1,0:T(8,128)(2,1)S(1)}, u32[]{:S(2)}, u32[]{:S(2)}) collective-permute-start(bf16[3,64,384]{2,1,0:T(8,128)(2,1)S(1)} %slice.8), channel_id=1, source_target_pairs={{1,0},{2,1},{3,2},{4,3},{5,4},{6,5},{7,6},{0,7},{9,8},{10,9},{11,1... | collective-permute-start | bytes 442376 | tf_op jit(solution)/shard_map/exchange/ppermute | solution.py:40
  77.5 16.9 %attend_next.3 = (f32[3,80,1536]{2,1,0:T(8,128)S(1)}, f32[3,8,1536]{2,1,0:T(8,128)S(1)}, f32[8,128]{1,0:T(8,128)S(1)}) custom-call(bf16[3,128,384]{2,1,0:T(8,128)(2,1)S(1)} %collective-permute-done.9.refs_0_, bf16[3,128,384]{2,1,0:T(8,128)(2,1)S(1)} %collective-permute-done.13.refs_1_, ...), custom_call_target="tpu_custom_call", output_to_operand_aliasing={{0}: (4, {}), {1}: (5, {}), {2}: (6, {})} | custom-call | flops 8847360000 | bytes 3407872 | tf_op jit(solution)/shard_map/attend/attend_next/pallas_call | solution.py:54
  94.5 15.2 %attend_last.1 = (f32[3,80,384]{2,1,0:T(8,128)S(1)}, f32[3,8,384]{2,1,0:T(8,128)S(1)}, f32[8,128]{1,0:T(8,128)S(1)}, bf16[208,384]{1,0:T(8,128)(2,1)}, bf16[208,...) custom-call(bf16[3,64,384]{2,1,0:T(8,128)(2,1)S(1)} %collective-permute-done.10.k_ref, ...), custom_call_target="tpu_custom_call" | custom-call | flops 4423680000 | bytes 3112960 | tf_op jit(solution)/shard_map/attend/attend_last/pallas_call | solution.py:54
  110.2 2.1 %collective-permute-start.19 = (bf16[208,384]{1,0:T(8,128)(2,1)}, bf16[208,384]{1,0:T(8,128)(2,1)S(1)}, u32[]{:S(2)}, u32[]{:S(2)}) collective-permute-start(bf16[208,384]{1,0:T(8,128)(2,1)} %get-tuple-element.80), channel_id=1, source_target_pairs={{8,0},{9,1},{10,2},{11,3},{12,4},{13,5},{14,6},{15,7},{16,8},{17,9... | collective-permute-start | bytes 479240 | tf_op jit(solution)/shard_map/combine/ppermute | solution.py:40
  113.3 2.1 %copy.20 = bf16[192,8,2,384]{3,1,2,0:T(8,128)(2,1)S(1)} copy(bf16[192,8,2,384]{3,2,1,0:T(2,128)(2,1)} %bitcast.11) | data formatting | bytes 4718592
  117.9 3.9 %attend_text.1 = (f32[3,80,384]{2,1,0:T(8,128)S(1)}, f32[3,8,384]{2,1,0:T(8,128)S(1)}, f32[8,128]{1,0:T(8,128)S(1)}) custom-call(bf16[3,128,384]{2,1,0:T(8,128)(2,1)S(1)} %text_project.1.refs_0_, bf16[3,128,1536]{2,1,0:T(8,128)(2,1)S(1)} %copy-done.7, ...), custom_call_target="tpu_custom_call", output_to_operand_aliasing={{0}: (3, {}), {1}: (4, {}), {2}: (5, {})} | custom-call | flops 1105920000 | bytes 1896448 | tf_op jit(solution)/shard_map/text/attend_text/pallas_call | solution.py:54
  122.1 1.5 %collective-permute-start.21 = (bf16[96,192]{1,0:T(8,128)(2,1)S(1)}, bf16[96,192]{1,0:T(8,128)(2,1)S(1)}, u32[]{:S(2)}, u32[]{:S(2)}) collective-permute-start(bf16[96,192]{1,0:T(8,128)(2,1)S(1)} %get-tuple-element.82), channel_id=1, source_target_pairs={{160,0},{161,1},{162,2},{163,3},{164,4},{165,5},{166,6},{167,7},{1... | collective-permute-start | bytes 110600 | tf_op jit(solution)/shard_map/output/ppermute | solution.py:40
  123.6 1.3 collective-permute-start.22
  126.5 3.1 %collective-permute-done.23.across = bf16[96,192]{1,0:T(8,128)(2,1)S(1)} collective-permute-done((bf16[96,192]{1,0:T(8,128)(2,1)S(1)}, bf16[96,192]{1,0:T(8,128)(2,1)S(1)}, u32[]{:S(2)}, u32[]{:S(2)}) %collective-permute-start.23) | collective-permute-done | bytes 36896 | tf_op jit(solution)/shard_map/output/ppermute | solution.py:40
  130.5 5.1 %collective-permute-start.25 = (bf16[48,1536]{1,0:T(8,128)(2,1)S(1)}, bf16[48,1536]{1,0:T(8,128)(2,1)S(1)}, u32[]{:S(2)}, u32[]{:S(2)}) collective-permute-start(bf16[48,1536]{1,0:T(8,128)(2,1)S(1)} %get-tuple-element.92), channel_id=1, source_target_pairs={{64,0},{65,1},{66,2},{67,3},{68,4},{69,5},{70,6},{71,7},{72,8},{73... | collective-permute-start | bytes 442376 | tf_op jit(solution)/shard_map/output/ppermute | solution.py:40
  (65 shorter events, 14.2 us)
Async XLA Ops:
  0.0 9.9 %collective-permute-start = (bf16[48,1536]{1,0:T(8,128)(2,1)}, bf16[48,1536]{1,0:T(8,128)(2,1)}, u32[]{:S(2)}, u32[]{:S(2)}) collective-permute-start(bf16[48,1536]{1,0:T(8,128)(2,1)} %refs_0_), channel_id=1, source_target_pairs={{128,0},{129,1},{130,2},{131,3},{132,4},{133,5},{134,6},{135,7},{1... | collective-permute-start | bytes 442376 | tf_op jit(solution)/shard_map/tokens/ppermute | solution.py:40
  3.3 7.5 %collective-permute-start.1 = (bf16[48,1536]{1,0:T(8,128)(2,1)}, bf16[48,1536]{1,0:T(8,128)(2,1)}, u32[]{:S(2)}, u32[]{:S(2)}) collective-permute-start(bf16[48,1536]{1,0:T(8,128)(2,1)} %refs_0_), channel_id=1, source_target_pairs={{160,0},{161,1},{162,2},{163,3},{164,4},{165,5},{166,6},{167,7},{1... | collective-permute-start | bytes 442376 | tf_op jit(solution)/shard_map/tokens/ppermute | solution.py:40
  3.3 8.1 %collective-permute-start.2 = (bf16[48,1536]{1,0:T(8,128)(2,1)}, bf16[48,1536]{1,0:T(8,128)(2,1)}, u32[]{:S(2)}, u32[]{:S(2)}) collective-permute-start(bf16[48,1536]{1,0:T(8,128)(2,1)} %refs_0_), channel_id=1, source_target_pairs={{32,0},{33,1},{34,2},{35,3},{36,4},{37,5},{38,6},{39,7},{40,8},{41... | collective-permute-start | bytes 442376 | tf_op jit(solution)/shard_map/tokens/ppermute | solution.py:40
  5.0 9.7 %collective-permute-start.3 = (bf16[48,1536]{1,0:T(8,128)(2,1)}, bf16[48,1536]{1,0:T(8,128)(2,1)}, u32[]{:S(2)}, u32[]{:S(2)}) collective-permute-start(bf16[48,1536]{1,0:T(8,128)(2,1)} %refs_0_), channel_id=1, source_target_pairs={{64,0},{65,1},{66,2},{67,3},{68,4},{69,5},{70,6},{71,7},{72,8},{73... | collective-permute-start | bytes 442376 | tf_op jit(solution)/shard_map/project/ppermute | solution.py:40
  11.4 4.0 %collective-permute-start.4 = (bf16[48,1536]{1,0:T(8,128)(2,1)}, bf16[48,1536]{1,0:T(8,128)(2,1)S(1)}, u32[]{:S(2)}, u32[]{:S(2)}) collective-permute-start(bf16[48,1536]{1,0:T(8,128)(2,1)} %collective-permute-done.refs_1_), channel_id=1, source_target_pairs={{64,0},{65,1},{66,2},{67,3},{68,4},{69,5},{70,6},{71,7},{72,8},{73... | collective-permute-start | bytes 442376 | tf_op jit(solution)/shard_map/project/ppermute | solution.py:40
  18.4 11.8 %collective-permute-start.7 = (bf16[3,128,384]{2,1,0:T(8,128)(2,1)S(1)}, bf16[3,128,384]{2,1,0:T(8,128)(2,1)S(1)}, u32[]{:S(2)}, u32[]{:S(2)}) collective-permute-start(bf16[3,128,384]{2,1,0:T(8,128)(2,1)S(1)} %get-tuple-element.54.refs_4_), channel_id=1, source_target_pairs={{1,0},{2,1},{3,2},{4,3},{5,4},{6,5},{7,6},{0,7},{9,8},{10,9},{11,1... | collective-permute-start | bytes 884744 | tf_op jit(solution)/shard_map/exchange/ppermute | solution.py:40
  24.0 9.5 %collective-permute-start.11 = (bf16[3,128,384]{2,1,0:T(8,128)(2,1)S(1)}, bf16[3,128,384]{2,1,0:T(8,128)(2,1)S(1)}, u32[]{:S(2)}, u32[]{:S(2)}) collective-permute-start(bf16[3,128,384]{2,1,0:T(8,128)(2,1)S(1)} %get-tuple-element.54.refs_4_), channel_id=1, source_target_pairs={{7,0},{0,1},{1,2},{2,3},{3,4},{4,5},{5,6},{6,7},{15,8},{8,9},{9,10... | collective-permute-start | bytes 884744 | tf_op jit(solution)/shard_map/exchange/ppermute | solution.py:40
  24.0 9.5 %collective-permute-start.15 = (bf16[3,64,384]{2,1,0:T(8,128)(2,1)S(1)}, bf16[3,64,384]{2,1,0:T(8,128)(2,1)S(1)}, u32[]{:S(2)}, u32[]{:S(2)}) collective-permute-start(bf16[3,64,384]{2,1,0:T(8,128)(2,1)S(1)} %get-tuple-element.55.refs_0_), channel_id=1, source_target_pairs={{8,0},{9,1},{10,2},{11,3},{12,4},{13,5},{14,6},{15,7},{16,8},{17,9... | collective-permute-start | bytes 442376 | tf_op jit(solution)/shard_map/exchange/ppermute | solution.py:40
  26.8 7.3 %collective-permute-start.16 = (bf16[3,64,384]{2,1,0:T(8,128)(2,1)S(1)}, bf16[3,64,384]{2,1,0:T(8,128)(2,1)S(1)}, u32[]{:S(2)}, u32[]{:S(2)}) collective-permute-start(bf16[3,64,384]{2,1,0:T(8,128)(2,1)S(1)} %get-tuple-element.55.refs_0_), channel_id=1, source_target_pairs={{24,0},{25,1},{26,2},{27,3},{28,4},{29,5},{30,6},{31,7},{0,8},{1,9... | collective-permute-start | bytes 442376 | tf_op jit(solution)/shard_map/exchange/ppermute | solution.py:40
  26.8 7.8 %collective-permute-start.17 = (bf16[3,64,384]{2,1,0:T(8,128)(2,1)S(1)}, bf16[3,64,384]{2,1,0:T(8,128)(2,1)S(1)}, u32[]{:S(2)}, u32[]{:S(2)}) collective-permute-start(bf16[3,64,384]{2,1,0:T(8,128)(2,1)S(1)} %get-tuple-element.55.refs_0_), channel_id=1, source_target_pairs={{16,0},{17,1},{18,2},{19,3},{20,4},{21,5},{22,6},{23,7},{24,8},{25... | collective-permute-start | bytes 442376 | tf_op jit(solution)/shard_map/exchange/ppermute | solution.py:40
  30.2 25.0 %collective-permute-start.8 = (bf16[3,128,384]{2,1,0:T(8,128)(2,1)S(1)}, bf16[3,128,384]{2,1,0:T(8,128)(2,1)S(1)}, u32[]{:S(2)}, u32[]{:S(2)}) collective-permute-start(bf16[3,128,384]{2,1,0:T(8,128)(2,1)S(1)} %collective-permute-done.7.refs_5_), channel_id=1, source_target_pairs={{1,0},{2,1},{3,2},{4,3},{5,4},{6,5},{7,6},{0,7},{9,8},{10,9},{11,1... | collective-permute-start | bytes 884744 | tf_op jit(solution)/shard_map/exchange/ppermute | solution.py:40
  33.6 24.1 %collective-permute-start.12 = (bf16[3,128,384]{2,1,0:T(8,128)(2,1)S(1)}, bf16[3,128,384]{2,1,0:T(8,128)(2,1)S(1)}, u32[]{:S(2)}, u32[]{:S(2)}) collective-permute-start(bf16[3,128,384]{2,1,0:T(8,128)(2,1)S(1)} %collective-permute-done.11.refs_6_), channel_id=1, source_target_pairs={{7,0},{0,1},{1,2},{2,3},{3,4},{4,5},{5,6},{6,7},{15,8},{8,9},{9,10... | collective-permute-start | bytes 884744 | tf_op jit(solution)/shard_map/exchange/ppermute | solution.py:40
  55.1 74.5 %collective-permute-start.24 = (bf16[384,1536]{1,0:T(8,128)(2,1)S(1)}, bf16[384,1536]{1,0:T(8,128)(2,1)S(1)}, u32[]{:S(2)}, u32[]{:S(2)}) collective-permute-start(bf16[384,1536]{1,0:T(8,128)(2,1)S(1)} %copy-done), channel_id=1, source_target_pairs={{0,128},{1,129},{2,130},{3,131},{4,132},{5,133},{6,134},{7,135},{8... | collective-permute-start | bytes 3538952 | tf_op jit(solution)/shard_map/exchange/ppermute | solution.py:47
  55.2 19.4 %collective-permute-start.9 = (bf16[3,128,384]{2,1,0:T(8,128)(2,1)S(1)}, bf16[3,128,384]{2,1,0:T(8,128)(2,1)S(1)}, u32[]{:S(2)}, u32[]{:S(2)}) collective-permute-start(bf16[3,128,384]{2,1,0:T(8,128)(2,1)S(1)} %collective-permute-done.8.refs_0_), channel_id=1, source_target_pairs={{1,0},{2,1},{3,2},{4,3},{5,4},{6,5},{7,6},{0,7},{9,8},{10,9},{11,1... | collective-permute-start | bytes 884744 | tf_op jit(solution)/shard_map/exchange/ppermute | solution.py:40
  57.7 19.7 %collective-permute-start.13 = (bf16[3,128,384]{2,1,0:T(8,128)(2,1)S(1)}, bf16[3,128,384]{2,1,0:T(8,128)(2,1)S(1)}, u32[]{:S(2)}, u32[]{:S(2)}) collective-permute-start(bf16[3,128,384]{2,1,0:T(8,128)(2,1)S(1)} %collective-permute-done.12.refs_1_), channel_id=1, source_target_pairs={{7,0},{0,1},{1,2},{2,3},{3,4},{4,5},{5,6},{6,7},{15,8},{8,9},{9,10... | collective-permute-start | bytes 884744 | tf_op jit(solution)/shard_map/exchange/ppermute | solution.py:40
  74.7 19.8 %collective-permute-start.10 = (bf16[3,64,384]{2,1,0:T(8,128)(2,1)S(1)}, bf16[3,64,384]{2,1,0:T(8,128)(2,1)S(1)}, u32[]{:S(2)}, u32[]{:S(2)}) collective-permute-start(bf16[3,64,384]{2,1,0:T(8,128)(2,1)S(1)} %slice.8), channel_id=1, source_target_pairs={{1,0},{2,1},{3,2},{4,3},{5,4},{6,5},{7,6},{0,7},{9,8},{10,9},{11,1... | collective-permute-start | bytes 442376 | tf_op jit(solution)/shard_map/exchange/ppermute | solution.py:40
  77.4 17.0 %collective-permute-start.14 = (bf16[3,64,384]{2,1,0:T(8,128)(2,1)S(1)}, bf16[3,64,384]{2,1,0:T(8,128)(2,1)S(1)}, u32[]{:S(2)}, u32[]{:S(2)}) collective-permute-start(bf16[3,64,384]{2,1,0:T(8,128)(2,1)S(1)} %slice.9), channel_id=1, source_target_pairs={{7,0},{0,1},{1,2},{2,3},{3,4},{4,5},{5,6},{6,7},{15,8},{8,9},{9,10... | collective-permute-start | bytes 442376 | tf_op jit(solution)/shard_map/exchange/ppermute | solution.py:40
  109.7 12.1 %collective-permute-start.18 = (bf16[208,384]{1,0:T(8,128)(2,1)}, bf16[208,384]{1,0:T(8,128)(2,1)S(1)}, u32[]{:S(2)}, u32[]{:S(2)}) collective-permute-start(bf16[208,384]{1,0:T(8,128)(2,1)} %get-tuple-element.79), channel_id=1, source_target_pairs={{24,0},{25,1},{26,2},{27,3},{28,4},{29,5},{30,6},{31,7},{0,8},{1,9... | collective-permute-start | bytes 479240 | tf_op jit(solution)/shard_map/combine/ppermute | solution.py:40
  110.2 11.6 %collective-permute-start.19 = (bf16[208,384]{1,0:T(8,128)(2,1)}, bf16[208,384]{1,0:T(8,128)(2,1)S(1)}, u32[]{:S(2)}, u32[]{:S(2)}) collective-permute-start(bf16[208,384]{1,0:T(8,128)(2,1)} %get-tuple-element.80), channel_id=1, source_target_pairs={{8,0},{9,1},{10,2},{11,3},{12,4},{13,5},{14,6},{15,7},{16,8},{17,9... | collective-permute-start | bytes 479240 | tf_op jit(solution)/shard_map/combine/ppermute | solution.py:40
  112.3 9.5 %collective-permute-start.20 = (bf16[208,384]{1,0:T(8,128)(2,1)S(1)}, bf16[208,384]{1,0:T(8,128)(2,1)S(1)}, u32[]{:S(2)}, u32[]{:S(2)}) collective-permute-start(bf16[208,384]{1,0:T(8,128)(2,1)S(1)} %get-tuple-element.81), channel_id=1, source_target_pairs={{16,0},{17,1},{18,2},{19,3},{20,4},{21,5},{22,6},{23,7},{24,8},{25... | collective-permute-start | bytes 479240 | tf_op jit(solution)/shard_map/combine/ppermute | solution.py:40
  122.1 4.2 %collective-permute-start.21 = (bf16[96,192]{1,0:T(8,128)(2,1)S(1)}, bf16[96,192]{1,0:T(8,128)(2,1)S(1)}, u32[]{:S(2)}, u32[]{:S(2)}) collective-permute-start(bf16[96,192]{1,0:T(8,128)(2,1)S(1)} %get-tuple-element.82), channel_id=1, source_target_pairs={{160,0},{161,1},{162,2},{163,3},{164,4},{165,5},{166,6},{167,7},{1... | collective-permute-start | bytes 110600 | tf_op jit(solution)/shard_map/output/ppermute | solution.py:40
  123.6 2.9 %collective-permute-start.22 = (bf16[96,192]{1,0:T(8,128)(2,1)S(1)}, bf16[96,192]{1,0:T(8,128)(2,1)S(1)}, u32[]{:S(2)}, u32[]{:S(2)}) collective-permute-start(bf16[96,192]{1,0:T(8,128)(2,1)S(1)} %get-tuple-element.83), channel_id=1, source_target_pairs={{128,0},{129,1},{130,2},{131,3},{132,4},{133,5},{134,6},{135,7},{1... | collective-permute-start | bytes 110600 | tf_op jit(solution)/shard_map/output/ppermute | solution.py:40
  124.9 4.7 %collective-permute-start.23 = (bf16[96,192]{1,0:T(8,128)(2,1)S(1)}, bf16[96,192]{1,0:T(8,128)(2,1)S(1)}, u32[]{:S(2)}, u32[]{:S(2)}) collective-permute-start(bf16[96,192]{1,0:T(8,128)(2,1)S(1)} %get-tuple-element.84), channel_id=1, source_target_pairs={{32,0},{33,1},{34,2},{35,3},{36,4},{37,5},{38,6},{39,7},{40,8},{41... | collective-permute-start | bytes 110600 | tf_op jit(solution)/shard_map/output/ppermute | solution.py:40
  130.5 6.1 %collective-permute-start.25 = (bf16[48,1536]{1,0:T(8,128)(2,1)S(1)}, bf16[48,1536]{1,0:T(8,128)(2,1)S(1)}, u32[]{:S(2)}, u32[]{:S(2)}) collective-permute-start(bf16[48,1536]{1,0:T(8,128)(2,1)S(1)} %get-tuple-element.92), channel_id=1, source_target_pairs={{64,0},{65,1},{66,2},{67,3},{68,4},{69,5},{70,6},{71,7},{72,8},{73... | collective-permute-start | bytes 442376 | tf_op jit(solution)/shard_map/output/ppermute | solution.py:40
  (11 other events, 104.1 us)

commit v2 on v1

--- a/solution.py
+++ b/solution.py
@@ -11,7 +11,7 @@
 AXES = ("uly", "blk")
 X, CORE, Y, Z = 4, 2, 4, 8
 ONES = 16
-VMEM_BYTES = 16 << 20
+VMEM_BYTES = 8 << 20
 STATS = 16
 LOG2_SCALE = 1.4426950408889634 * HEAD_DIM**-0.5
 SAFE_SQUARE = 96.0**2
@@ -289,9 +289,9 @@
     out_ref[...] = out_rows(piece, w_ref, high_ref[0])
 
 
-def far_kernel(high_ref, near_ref, up, down, across, w_ref, w_side_ref, kept_ref, sent_ref):
-    total = near_ref[...] + out_rows(across, w_ref, high_ref[2])
-    total = total + out_rows(up, w_side_ref, high_ref[0]) + out_rows(down, w_side_ref, high_ref[1])
+def far_kernel(high_ref, near_ref, across, up, down, w_ref, w_side_ref, kept_ref, sent_ref):
+    total = near_ref[...] + out_rows(across, w_ref, high_ref[0])
+    total = total + out_rows(up, w_side_ref, high_ref[1]) + out_rows(down, w_side_ref, high_ref[2])
     half = kept_ref.shape[0]
     kept_ref[...] = total[:half]
     sent_ref[...] = total[half:].astype(BF16)
@@ -453,8 +453,8 @@
         pieces = call(combine_kernel, (piece,) * X, 0, acc, m, *returned, name="combine")
 
     with jax.named_scope("output"):
-        distances = (1, -1, 2)
-        received = [fetch(p, dx=-d) for p, d in zip(pieces[1:], distances)]
+        distances = (2, 1, -1)
+        received = [fetch(pieces[at], dx=-d) for at, d in zip((3, 1, 2), distances)]
         flops = 2 * CORE * block * width * model_width
         total = call(
             near_kernel,

time: 138 us -> 136 us (0.986)
  waiting for transfers between devices: 10.4 us -> 7.74 us
    ppermute x25, waiting for transfers between devices: 10.4 us -> 7.74 us  [fetch(): return lax.ppermute(array, AXES, pairs)]
  transfers between devices with their start and end apart: 26 -> 26, of which waited for: 12 -> 11; matrix products, arithmetic and copies ran while one was open for 3% -> 3% of each run, Pallas kernels for 56% -> 56%
where the time goes in v2:
time: 136 us; the launch traced here: 135 us
  Pallas kernels  80.4 us (59%)
  starting transfers between devices  41.6 us (31%)
  waiting for transfers between devices  7.74 us (6%)
  local copies, waits for them, and re-layouts  5.41 us (4%)
    pallas_call x13, Pallas kernels, call(): pl.pallas_call(kernel, out_shape=out_shape, in_specs=[scalar_spec] * len(...  80.4 us
    ppermute x25, starting transfers between devices, fetch(): return lax.ppermute(array, AXES, pairs)  41.5 us
    ppermute x25, waiting for transfers between devices, fetch(): return lax.ppermute(array, AXES, pairs)  7.74 us
    unnamed x20, local copies, waits for them, and re-layouts  5.37 us
  transfers between devices with their start and end apart: 26, of which 11 were waited for; matrix products, arithmetic and copies ran while one was open for 3% of the time, Pallas kernels for 56%

profile of v2, /device:TPU:1, one launch (start us, length us, event | category | flops | bytes accessed | tf_op | source)
XLA Modules:
  0.0 135.5 jit_solution(12818654162061134671)
XLA Ops:
  0.0 3.3 %collective-permute-start = (bf16[48,1536]{1,0:T(8,128)(2,1)}, bf16[48,1536]{1,0:T(8,128)(2,1)}, u32[]{:S(2)}, u32[]{:S(2)}) collective-permute-start(bf16[48,1536]{1,0:T(8,128)(2,1)} %refs_0_), channel_id=1, source_target_pairs={{128,0},{129,1},{130,2},{131,3},{132,4},{133,5},{134,6},{135,7},{1... | collective-permute-start | bytes 442376 | tf_op jit(solution)/shard_map/tokens/ppermute | solution.py:40
  3.3 1.7 %collective-permute-start.2 = (bf16[48,1536]{1,0:T(8,128)(2,1)}, bf16[48,1536]{1,0:T(8,128)(2,1)}, u32[]{:S(2)}, u32[]{:S(2)}) collective-permute-start(bf16[48,1536]{1,0:T(8,128)(2,1)} %refs_0_), channel_id=1, source_target_pairs={{32,0},{33,1},{34,2},{35,3},{36,4},{37,5},{38,6},{39,7},{40,8},{41... | collective-permute-start | bytes 442376 | tf_op jit(solution)/shard_map/tokens/ppermute | solution.py:40
  5.0 1.5 %collective-permute-start.3 = (bf16[48,1536]{1,0:T(8,128)(2,1)}, bf16[48,1536]{1,0:T(8,128)(2,1)}, u32[]{:S(2)}, u32[]{:S(2)}) collective-permute-start(bf16[48,1536]{1,0:T(8,128)(2,1)} %refs_0_), channel_id=1, source_target_pairs={{64,0},{65,1},{66,2},{67,3},{68,4},{69,5},{70,6},{71,7},{72,8},{73... | collective-permute-start | bytes 442376 | tf_op jit(solution)/shard_map/project/ppermute | solution.py:40
  6.6 2.2 %copy.19 = bf16[192,8,2,384]{3,1,2,0:T(8,128)(2,1)S(1)} copy(bf16[192,8,2,384]{3,2,1,0:T(2,128)(2,1)} %bitcast.10) | data formatting | bytes 4718592
  8.8 1.1 halves.2.w_ref
  11.4 2.8 %collective-permute-start.4 = (bf16[48,1536]{1,0:T(8,128)(2,1)}, bf16[48,1536]{1,0:T(8,128)(2,1)S(1)}, u32[]{:S(2)}, u32[]{:S(2)}) collective-permute-start(bf16[48,1536]{1,0:T(8,128)(2,1)} %collective-permute-done.refs_1_), channel_id=1, source_target_pairs={{64,0},{65,1},{66,2},{67,3},{68,4},{69,5},{70,6},{71,7},{72,8},{73... | collective-permute-start | bytes 442376 | tf_op jit(solution)/shard_map/project/ppermute | solution.py:40
  16.1 2.3 %project.1 = (bf16[3,64,384]{2,1,0:T(8,128)(2,1)S(1)}, bf16[3,128,384]{2,1,0:T(8,128)(2,1)S(1)}) custom-call(s32[1]{0:T(128)} %bitcast.3.high_ref, bf16[1536,576]{1,0:T(8,128)(2,1)S(1)} %halves.2.w_ref, f32[3,384]{1,0:T(4,128)S(1)} %copy-done.4, bf16[48,1536]{1,0:T(8,128)(2,1)S(1)} %copy-done.3, bf16[48,1536]{1,0:T(8,128)(2,1)} %collective-permute-done.refs_1_, ...), custom_call_target="tpu_custom_call" | custom-call | flops 679477248 | bytes 2953728 | tf_op jit(solution)/shard_map/project/project/pallas_call | solution.py:54
  18.4 5.7 %collective-permute-start.7 = (bf16[3,128,384]{2,1,0:T(8,128)(2,1)S(1)}, bf16[3,128,384]{2,1,0:T(8,128)(2,1)S(1)}, u32[]{:S(2)}, u32[]{:S(2)}) collective-permute-start(bf16[3,128,384]{2,1,0:T(8,128)(2,1)S(1)} %get-tuple-element.54.refs_4_), channel_id=1, source_target_pairs={{1,0},{2,1},{3,2},{4,3},{5,4},{6,5},{7,6},{0,7},{9,8},{10,9},{11,1... | collective-permute-start | bytes 884744 | tf_op jit(solution)/shard_map/exchange/ppermute | solution.py:40
  24.0 2.7 %collective-permute-start.15 = (bf16[3,64,384]{2,1,0:T(8,128)(2,1)S(1)}, bf16[3,64,384]{2,1,0:T(8,128)(2,1)S(1)}, u32[]{:S(2)}, u32[]{:S(2)}) collective-permute-start(bf16[3,64,384]{2,1,0:T(8,128)(2,1)S(1)} %get-tuple-element.55.refs_0_), channel_id=1, source_target_pairs={{8,0},{9,1},{10,2},{11,3},{12,4},{13,5},{14,6},{15,7},{16,8},{17,9... | collective-permute-start | bytes 442376 | tf_op jit(solution)/shard_map/exchange/ppermute | solution.py:40
  26.8 1.6 %collective-permute-start.17 = (bf16[3,64,384]{2,1,0:T(8,128)(2,1)S(1)}, bf16[3,64,384]{2,1,0:T(8,128)(2,1)S(1)}, u32[]{:S(2)}, u32[]{:S(2)}) collective-permute-start(bf16[3,64,384]{2,1,0:T(8,128)(2,1)S(1)} %get-tuple-element.55.refs_0_), channel_id=1, source_target_pairs={{16,0},{17,1},{18,2},{19,3},{20,4},{21,5},{22,6},{23,7},{24,8},{25... | collective-permute-start | bytes 442376 | tf_op jit(solution)/shard_map/exchange/ppermute | solution.py:40
  28.4 1.7 %collective-permute-done.7.refs_5_ = bf16[3,128,384]{2,1,0:T(8,128)(2,1)S(1)} collective-permute-done((bf16[3,128,384]{2,1,0:T(8,128)(2,1)S(1)}, bf16[3,128,384]{2,1,0:T(8,128)(2,1)S(1)}, u32[]{:S(2)}, u32[]{:S(2)}) %collective-permute-start.7) | collective-permute-done | bytes 294944 | tf_op jit(solution)/shard_map/exchange/ppermute | solution.py:40
  30.2 3.4 %collective-permute-start.8 = (bf16[3,128,384]{2,1,0:T(8,128)(2,1)S(1)}, bf16[3,128,384]{2,1,0:T(8,128)(2,1)S(1)}, u32[]{:S(2)}, u32[]{:S(2)}) collective-permute-start(bf16[3,128,384]{2,1,0:T(8,128)(2,1)S(1)} %collective-permute-done.7.refs_5_), channel_id=1, source_target_pairs={{1,0},{2,1},{3,2},{4,3},{5,4},{6,5},{7,6},{0,7},{9,8},{10,9},{11,1... | collective-permute-start | bytes 884744 | tf_op jit(solution)/shard_map/exchange/ppermute | solution.py:40
  34.6 20.5 %attend_first.1 = (f32[3,80,1536]{2,1,0:T(8,128)S(1)}, f32[3,8,1536]{2,1,0:T(8,128)S(1)}, f32[8,128]{1,0:T(8,128)S(1)}, bf16[3,128,1536]{2,1,0:T(8,128)(2,1)S(1)}, f32[3,8,128]{2,1,0:T(8,128)S(1)}) custom-call(bf16[3,64,384]{2,1,0:T(8,128)(2,1)S(1)} %get-tuple-element.55.refs_0_, bf16[3,64,384]{2,1,0:T(8,128)(2,1)S(1)} %collective-permute-done.15.refs_1_, ...), custom_call_target="tpu_custom_call" | custom-call | flops 13271040000 | bytes 1474560 | tf_op jit(solution)/shard_map/attend/attend_first/pallas_call | solution.py:54
  55.2 2.5 %collective-permute-start.9 = (bf16[3,128,384]{2,1,0:T(8,128)(2,1)S(1)}, bf16[3,128,384]{2,1,0:T(8,128)(2,1)S(1)}, u32[]{:S(2)}, u32[]{:S(2)}) collective-permute-start(bf16[3,128,384]{2,1,0:T(8,128)(2,1)S(1)} %collective-permute-done.8.refs_0_), channel_id=1, source_target_pairs={{1,0},{2,1},{3,2},{4,3},{5,4},{6,5},{7,6},{0,7},{9,8},{10,9},{11,1... | collective-permute-start | bytes 884744 | tf_op jit(solution)/shard_map/exchange/ppermute | solution.py:40
  57.7 16.9 %attend_next.2 = (f32[3,80,1536]{2,1,0:T(8,128)S(1)}, f32[3,8,1536]{2,1,0:T(8,128)S(1)}, f32[8,128]{1,0:T(8,128)S(1)}) custom-call(bf16[3,128,384]{2,1,0:T(8,128)(2,1)S(1)} %collective-permute-done.8.refs_0_, bf16[3,128,384]{2,1,0:T(8,128)(2,1)S(1)} %collective-permute-done.12.refs_1_, ...), custom_call_target="tpu_custom_call", output_to_operand_aliasing={{0}: (4, {}), {1}: (5, {}), {2}: (6, {})} | custom-call | flops 8847360000 | bytes 3407872 | tf_op jit(solution)/shard_map/attend/attend_next/pallas_call | solution.py:54
  74.7 2.7 %collective-permute-start.10 = (bf16[3,64,384]{2,1,0:T(8,128)(2,1)S(1)}, bf16[3,64,384]{2,1,0:T(8,128)(2,1)S(1)}, u32[]{:S(2)}, u32[]{:S(2)}) collective-permute-start(bf16[3,64,384]{2,1,0:T(8,128)(2,1)S(1)} %slice.8), channel_id=1, source_target_pairs={{1,0},{2,1},{3,2},{4,3},{5,4},{6,5},{7,6},{0,7},{9,8},{10,9},{11,1... | collective-permute-start | bytes 442376 | tf_op jit(solution)/shard_map/exchange/ppermute | solution.py:40
  77.5 16.9 %attend_next.3 = (f32[3,80,1536]{2,1,0:T(8,128)S(1)}, f32[3,8,1536]{2,1,0:T(8,128)S(1)}, f32[8,128]{1,0:T(8,128)S(1)}) custom-call(bf16[3,128,384]{2,1,0:T(8,128)(2,1)S(1)} %collective-permute-done.9.refs_0_, bf16[3,128,384]{2,1,0:T(8,128)(2,1)S(1)} %collective-permute-done.13.refs_1_, ...), custom_call_target="tpu_custom_call", output_to_operand_aliasing={{0}: (4, {}), {1}: (5, {}), {2}: (6, {})} | custom-call | flops 8847360000 | bytes 3407872 | tf_op jit(solution)/shard_map/attend/attend_next/pallas_call | solution.py:54
  94.5 15.2 %attend_last.1 = (f32[3,80,384]{2,1,0:T(8,128)S(1)}, f32[3,8,384]{2,1,0:T(8,128)S(1)}, f32[8,128]{1,0:T(8,128)S(1)}, bf16[208,384]{1,0:T(8,128)(2,1)}, bf16[208,...) custom-call(bf16[3,64,384]{2,1,0:T(8,128)(2,1)S(1)} %collective-permute-done.10.k_ref, ...), custom_call_target="tpu_custom_call" | custom-call | flops 4423680000 | bytes 3112960 | tf_op jit(solution)/shard_map/attend/attend_last/pallas_call | solution.py:54
  110.2 2.1 %collective-permute-start.19 = (bf16[208,384]{1,0:T(8,128)(2,1)}, bf16[208,384]{1,0:T(8,128)(2,1)S(1)}, u32[]{:S(2)}, u32[]{:S(2)}) collective-permute-start(bf16[208,384]{1,0:T(8,128)(2,1)} %get-tuple-element.80), channel_id=1, source_target_pairs={{8,0},{9,1},{10,2},{11,3},{12,4},{13,5},{14,6},{15,7},{16,8},{17,9... | collective-permute-start | bytes 479240 | tf_op jit(solution)/shard_map/combine/ppermute | solution.py:40
  113.3 2.1 %copy.20 = bf16[192,8,2,384]{3,1,2,0:T(8,128)(2,1)S(1)} copy(bf16[192,8,2,384]{3,2,1,0:T(2,128)(2,1)} %bitcast.11) | data formatting | bytes 4718592
  117.9 3.9 %attend_text.1 = (f32[3,80,384]{2,1,0:T(8,128)S(1)}, f32[3,8,384]{2,1,0:T(8,128)S(1)}, f32[8,128]{1,0:T(8,128)S(1)}) custom-call(bf16[3,128,384]{2,1,0:T(8,128)(2,1)S(1)} %text_project.1.refs_0_, bf16[3,128,1536]{2,1,0:T(8,128)(2,1)S(1)} %copy-done.7, ...), custom_call_target="tpu_custom_call", output_to_operand_aliasing={{0}: (3, {}), {1}: (4, {}), {2}: (5, {})} | custom-call | flops 1105920000 | bytes 1896448 | tf_op jit(solution)/shard_map/text/attend_text/pallas_call | solution.py:54
  122.1 1.2 collective-permute-start.21
  123.7 2.3 %collective-permute-start.23 = (bf16[96,192]{1,0:T(8,128)(2,1)S(1)}, bf16[96,192]{1,0:T(8,128)(2,1)S(1)}, u32[]{:S(2)}, u32[]{:S(2)}) collective-permute-start(bf16[96,192]{1,0:T(8,128)(2,1)S(1)} %get-tuple-element.84), channel_id=1, source_target_pairs={{128,0},{129,1},{130,2},{131,3},{132,4},{133,5},{134,6},{135,7},{1... | collective-permute-start | bytes 110600 | tf_op jit(solution)/shard_map/output/ppermute | solution.py:40
  128.4 5.4 %collective-permute-start.25 = (bf16[48,1536]{1,0:T(8,128)(2,1)S(1)}, bf16[48,1536]{1,0:T(8,128)(2,1)S(1)}, u32[]{:S(2)}, u32[]{:S(2)}) collective-permute-start(bf16[48,1536]{1,0:T(8,128)(2,1)S(1)} %get-tuple-element.92), channel_id=1, source_target_pairs={{64,0},{65,1},{66,2},{67,3},{68,4},{69,5},{70,6},{71,7},{72,8},{73... | collective-permute-start | bytes 442376 | tf_op jit(solution)/shard_map/output/ppermute | solution.py:40
  (65 shorter events, 13.3 us)
Async XLA Ops:
  0.0 9.9 %collective-permute-start = (bf16[48,1536]{1,0:T(8,128)(2,1)}, bf16[48,1536]{1,0:T(8,128)(2,1)}, u32[]{:S(2)}, u32[]{:S(2)}) collective-permute-start(bf16[48,1536]{1,0:T(8,128)(2,1)} %refs_0_), channel_id=1, source_target_pairs={{128,0},{129,1},{130,2},{131,3},{132,4},{133,5},{134,6},{135,7},{1... | collective-permute-start | bytes 442376 | tf_op jit(solution)/shard_map/tokens/ppermute | solution.py:40
  3.3 7.5 %collective-permute-start.1 = (bf16[48,1536]{1,0:T(8,128)(2,1)}, bf16[48,1536]{1,0:T(8,128)(2,1)}, u32[]{:S(2)}, u32[]{:S(2)}) collective-permute-start(bf16[48,1536]{1,0:T(8,128)(2,1)} %refs_0_), channel_id=1, source_target_pairs={{160,0},{161,1},{162,2},{163,3},{164,4},{165,5},{166,6},{167,7},{1... | collective-permute-start | bytes 442376 | tf_op jit(solution)/shard_map/tokens/ppermute | solution.py:40
  3.3 8.1 %collective-permute-start.2 = (bf16[48,1536]{1,0:T(8,128)(2,1)}, bf16[48,1536]{1,0:T(8,128)(2,1)}, u32[]{:S(2)}, u32[]{:S(2)}) collective-permute-start(bf16[48,1536]{1,0:T(8,128)(2,1)} %refs_0_), channel_id=1, source_target_pairs={{32,0},{33,1},{34,2},{35,3},{36,4},{37,5},{38,6},{39,7},{40,8},{41... | collective-permute-start | bytes 442376 | tf_op jit(solution)/shard_map/tokens/ppermute | solution.py:40
  5.0 9.7 %collective-permute-start.3 = (bf16[48,1536]{1,0:T(8,128)(2,1)}, bf16[48,1536]{1,0:T(8,128)(2,1)}, u32[]{:S(2)}, u32[]{:S(2)}) collective-permute-start(bf16[48,1536]{1,0:T(8,128)(2,1)} %refs_0_), channel_id=1, source_target_pairs={{64,0},{65,1},{66,2},{67,3},{68,4},{69,5},{70,6},{71,7},{72,8},{73... | collective-permute-start | bytes 442376 | tf_op jit(solution)/shard_map/project/ppermute | solution.py:40
  11.4 4.0 %collective-permute-start.4 = (bf16[48,1536]{1,0:T(8,128)(2,1)}, bf16[48,1536]{1,0:T(8,128)(2,1)S(1)}, u32[]{:S(2)}, u32[]{:S(2)}) collective-permute-start(bf16[48,1536]{1,0:T(8,128)(2,1)} %collective-permute-done.refs_1_), channel_id=1, source_target_pairs={{64,0},{65,1},{66,2},{67,3},{68,4},{69,5},{70,6},{71,7},{72,8},{73... | collective-permute-start | bytes 442376 | tf_op jit(solution)/shard_map/project/ppermute | solution.py:40
  18.4 11.8 %collective-permute-start.7 = (bf16[3,128,384]{2,1,0:T(8,128)(2,1)S(1)}, bf16[3,128,384]{2,1,0:T(8,128)(2,1)S(1)}, u32[]{:S(2)}, u32[]{:S(2)}) collective-permute-start(bf16[3,128,384]{2,1,0:T(8,128)(2,1)S(1)} %get-tuple-element.54.refs_4_), channel_id=1, source_target_pairs={{1,0},{2,1},{3,2},{4,3},{5,4},{6,5},{7,6},{0,7},{9,8},{10,9},{11,1... | collective-permute-start | bytes 884744 | tf_op jit(solution)/shard_map/exchange/ppermute | solution.py:40
  24.0 9.5 %collective-permute-start.11 = (bf16[3,128,384]{2,1,0:T(8,128)(2,1)S(1)}, bf16[3,128,384]{2,1,0:T(8,128)(2,1)S(1)}, u32[]{:S(2)}, u32[]{:S(2)}) collective-permute-start(bf16[3,128,384]{2,1,0:T(8,128)(2,1)S(1)} %get-tuple-element.54.refs_4_), channel_id=1, source_target_pairs={{7,0},{0,1},{1,2},{2,3},{3,4},{4,5},{5,6},{6,7},{15,8},{8,9},{9,10... | collective-permute-start | bytes 884744 | tf_op jit(solution)/shard_map/exchange/ppermute | solution.py:40
  24.0 9.5 %collective-permute-start.15 = (bf16[3,64,384]{2,1,0:T(8,128)(2,1)S(1)}, bf16[3,64,384]{2,1,0:T(8,128)(2,1)S(1)}, u32[]{:S(2)}, u32[]{:S(2)}) collective-permute-start(bf16[3,64,384]{2,1,0:T(8,128)(2,1)S(1)} %get-tuple-element.55.refs_0_), channel_id=1, source_target_pairs={{8,0},{9,1},{10,2},{11,3},{12,4},{13,5},{14,6},{15,7},{16,8},{17,9... | collective-permute-start | bytes 442376 | tf_op jit(solution)/shard_map/exchange/ppermute | solution.py:40
  26.8 7.3 %collective-permute-start.16 = (bf16[3,64,384]{2,1,0:T(8,128)(2,1)S(1)}, bf16[3,64,384]{2,1,0:T(8,128)(2,1)S(1)}, u32[]{:S(2)}, u32[]{:S(2)}) collective-permute-start(bf16[3,64,384]{2,1,0:T(8,128)(2,1)S(1)} %get-tuple-element.55.refs_0_), channel_id=1, source_target_pairs={{24,0},{25,1},{26,2},{27,3},{28,4},{29,5},{30,6},{31,7},{0,8},{1,9... | collective-permute-start | bytes 442376 | tf_op jit(solution)/shard_map/exchange/ppermute | solution.py:40
  26.8 7.8 %collective-permute-start.17 = (bf16[3,64,384]{2,1,0:T(8,128)(2,1)S(1)}, bf16[3,64,384]{2,1,0:T(8,128)(2,1)S(1)}, u32[]{:S(2)}, u32[]{:S(2)}) collective-permute-start(bf16[3,64,384]{2,1,0:T(8,128)(2,1)S(1)} %get-tuple-element.55.refs_0_), channel_id=1, source_target_pairs={{16,0},{17,1},{18,2},{19,3},{20,4},{21,5},{22,6},{23,7},{24,8},{25... | collective-permute-start | bytes 442376 | tf_op jit(solution)/shard_map/exchange/ppermute | solution.py:40
  30.2 25.0 %collective-permute-start.8 = (bf16[3,128,384]{2,1,0:T(8,128)(2,1)S(1)}, bf16[3,128,384]{2,1,0:T(8,128)(2,1)S(1)}, u32[]{:S(2)}, u32[]{:S(2)}) collective-permute-start(bf16[3,128,384]{2,1,0:T(8,128)(2,1)S(1)} %collective-permute-done.7.refs_5_), channel_id=1, source_target_pairs={{1,0},{2,1},{3,2},{4,3},{5,4},{6,5},{7,6},{0,7},{9,8},{10,9},{11,1... | collective-permute-start | bytes 884744 | tf_op jit(solution)/shard_map/exchange/ppermute | solution.py:40
  33.6 24.1 %collective-permute-start.12 = (bf16[3,128,384]{2,1,0:T(8,128)(2,1)S(1)}, bf16[3,128,384]{2,1,0:T(8,128)(2,1)S(1)}, u32[]{:S(2)}, u32[]{:S(2)}) collective-permute-start(bf16[3,128,384]{2,1,0:T(8,128)(2,1)S(1)} %collective-permute-done.11.refs_6_), channel_id=1, source_target_pairs={{7,0},{0,1},{1,2},{2,3},{3,4},{4,5},{5,6},{6,7},{15,8},{8,9},{9,10... | collective-permute-start | bytes 884744 | tf_op jit(solution)/shard_map/exchange/ppermute | solution.py:40
  55.1 72.3 %collective-permute-start.24 = (bf16[384,1536]{1,0:T(8,128)(2,1)S(1)}, bf16[384,1536]{1,0:T(8,128)(2,1)S(1)}, u32[]{:S(2)}, u32[]{:S(2)}) collective-permute-start(bf16[384,1536]{1,0:T(8,128)(2,1)S(1)} %copy-done), channel_id=1, source_target_pairs={{0,128},{1,129},{2,130},{3,131},{4,132},{5,133},{6,134},{7,135},{8... | collective-permute-start | bytes 3538952 | tf_op jit(solution)/shard_map/exchange/ppermute | solution.py:47
  55.2 19.4 %collective-permute-start.9 = (bf16[3,128,384]{2,1,0:T(8,128)(2,1)S(1)}, bf16[3,128,384]{2,1,0:T(8,128)(2,1)S(1)}, u32[]{:S(2)}, u32[]{:S(2)}) collective-permute-start(bf16[3,128,384]{2,1,0:T(8,128)(2,1)S(1)} %collective-permute-done.8.refs_0_), channel_id=1, source_target_pairs={{1,0},{2,1},{3,2},{4,3},{5,4},{6,5},{7,6},{0,7},{9,8},{10,9},{11,1... | collective-permute-start | bytes 884744 | tf_op jit(solution)/shard_map/exchange/ppermute | solution.py:40
  57.7 19.7 %collective-permute-start.13 = (bf16[3,128,384]{2,1,0:T(8,128)(2,1)S(1)}, bf16[3,128,384]{2,1,0:T(8,128)(2,1)S(1)}, u32[]{:S(2)}, u32[]{:S(2)}) collective-permute-start(bf16[3,128,384]{2,1,0:T(8,128)(2,1)S(1)} %collective-permute-done.12.refs_1_), channel_id=1, source_target_pairs={{7,0},{0,1},{1,2},{2,3},{3,4},{4,5},{5,6},{6,7},{15,8},{8,9},{9,10... | collective-permute-start | bytes 884744 | tf_op jit(solution)/shard_map/exchange/ppermute | solution.py:40
  74.7 19.8 %collective-permute-start.10 = (bf16[3,64,384]{2,1,0:T(8,128)(2,1)S(1)}, bf16[3,64,384]{2,1,0:T(8,128)(2,1)S(1)}, u32[]{:S(2)}, u32[]{:S(2)}) collective-permute-start(bf16[3,64,384]{2,1,0:T(8,128)(2,1)S(1)} %slice.8), channel_id=1, source_target_pairs={{1,0},{2,1},{3,2},{4,3},{5,4},{6,5},{7,6},{0,7},{9,8},{10,9},{11,1... | collective-permute-start | bytes 442376 | tf_op jit(solution)/shard_map/exchange/ppermute | solution.py:40
  77.4 17.0 %collective-permute-start.14 = (bf16[3,64,384]{2,1,0:T(8,128)(2,1)S(1)}, bf16[3,64,384]{2,1,0:T(8,128)(2,1)S(1)}, u32[]{:S(2)}, u32[]{:S(2)}) collective-permute-start(bf16[3,64,384]{2,1,0:T(8,128)(2,1)S(1)} %slice.9), channel_id=1, source_target_pairs={{7,0},{0,1},{1,2},{2,3},{3,4},{4,5},{5,6},{6,7},{15,8},{8,9},{9,10... | collective-permute-start | bytes 442376 | tf_op jit(solution)/shard_map/exchange/ppermute | solution.py:40
  109.7 12.1 %collective-permute-start.18 = (bf16[208,384]{1,0:T(8,128)(2,1)}, bf16[208,384]{1,0:T(8,128)(2,1)S(1)}, u32[]{:S(2)}, u32[]{:S(2)}) collective-permute-start(bf16[208,384]{1,0:T(8,128)(2,1)} %get-tuple-element.79), channel_id=1, source_target_pairs={{24,0},{25,1},{26,2},{27,3},{28,4},{29,5},{30,6},{31,7},{0,8},{1,9... | collective-permute-start | bytes 479240 | tf_op jit(solution)/shard_map/combine/ppermute | solution.py:40
  110.2 11.6 %collective-permute-start.19 = (bf16[208,384]{1,0:T(8,128)(2,1)}, bf16[208,384]{1,0:T(8,128)(2,1)S(1)}, u32[]{:S(2)}, u32[]{:S(2)}) collective-permute-start(bf16[208,384]{1,0:T(8,128)(2,1)} %get-tuple-element.80), channel_id=1, source_target_pairs={{8,0},{9,1},{10,2},{11,3},{12,4},{13,5},{14,6},{15,7},{16,8},{17,9... | collective-permute-start | bytes 479240 | tf_op jit(solution)/shard_map/combine/ppermute | solution.py:40
  112.3 9.5 %collective-permute-start.20 = (bf16[208,384]{1,0:T(8,128)(2,1)S(1)}, bf16[208,384]{1,0:T(8,128)(2,1)S(1)}, u32[]{:S(2)}, u32[]{:S(2)}) collective-permute-start(bf16[208,384]{1,0:T(8,128)(2,1)S(1)} %get-tuple-element.81), channel_id=1, source_target_pairs={{16,0},{17,1},{18,2},{19,3},{20,4},{21,5},{22,6},{23,7},{24,8},{25... | collective-permute-start | bytes 479240 | tf_op jit(solution)/shard_map/combine/ppermute | solution.py:40
  122.1 4.5 %collective-permute-start.21 = (bf16[96,192]{1,0:T(8,128)(2,1)S(1)}, bf16[96,192]{1,0:T(8,128)(2,1)S(1)}, u32[]{:S(2)}, u32[]{:S(2)}) collective-permute-start(bf16[96,192]{1,0:T(8,128)(2,1)S(1)} %get-tuple-element.82), channel_id=1, source_target_pairs={{32,0},{33,1},{34,2},{35,3},{36,4},{37,5},{38,6},{39,7},{40,8},{41... | collective-permute-start | bytes 110600 | tf_op jit(solution)/shard_map/output/ppermute | solution.py:40
  123.3 4.2 %collective-permute-start.22 = (bf16[96,192]{1,0:T(8,128)(2,1)S(1)}, bf16[96,192]{1,0:T(8,128)(2,1)S(1)}, u32[]{:S(2)}, u32[]{:S(2)}) collective-permute-start(bf16[96,192]{1,0:T(8,128)(2,1)S(1)} %get-tuple-element.83), channel_id=1, source_target_pairs={{160,0},{161,1},{162,2},{163,3},{164,4},{165,5},{166,6},{167,7},{1... | collective-permute-start | bytes 110600 | tf_op jit(solution)/shard_map/output/ppermute | solution.py:40
  123.7 3.8 %collective-permute-start.23 = (bf16[96,192]{1,0:T(8,128)(2,1)S(1)}, bf16[96,192]{1,0:T(8,128)(2,1)S(1)}, u32[]{:S(2)}, u32[]{:S(2)}) collective-permute-start(bf16[96,192]{1,0:T(8,128)(2,1)S(1)} %get-tuple-element.84), channel_id=1, source_target_pairs={{128,0},{129,1},{130,2},{131,3},{132,4},{133,5},{134,6},{135,7},{1... | collective-permute-start | bytes 110600 | tf_op jit(solution)/shard_map/output/ppermute | solution.py:40
  128.4 6.4 %collective-permute-start.25 = (bf16[48,1536]{1,0:T(8,128)(2,1)S(1)}, bf16[48,1536]{1,0:T(8,128)(2,1)S(1)}, u32[]{:S(2)}, u32[]{:S(2)}) collective-permute-start(bf16[48,1536]{1,0:T(8,128)(2,1)S(1)} %get-tuple-element.92), channel_id=1, source_target_pairs={{64,0},{65,1},{66,2},{67,3},{68,4},{69,5},{70,6},{71,7},{72,8},{73... | collective-permute-start | bytes 442376 | tf_op jit(solution)/shard_map/output/ppermute | solution.py:40
  (11 other events, 101.7 us)

commit v3 on v2

--- a/solution.py
+++ b/solution.py
@@ -357,8 +357,6 @@
         for _ in range(2):
             up.append(fetch(up[-1], dz=1))
             down.append(fetch(down[-1], dz=-1))
-        w_from, up[1] = lax.optimization_barrier((w_out, up[1]))
-        w_side = fetch_x_low(w_from)
         far_keys = fetch(up[-1][:, :HEAD_DIM], dz=1)
         far_values = fetch(down[-1][:, HEAD_DIM:], dz=-1)
 
@@ -403,6 +401,9 @@
                 aliases={n + 4: n for n in range(3)},
                 name="attend_next",
             )
+            if at == 1:
+                w_from, acc = lax.optimization_barrier((w_out, acc))
+                w_side = fetch_x_low(w_from)
         pack = shape((heads * HEAD_DIM + STATS, mine), BF16)
         acc, m, bound, *packs = call(
             functools.partial(last_kernel, 1536),

time: 136 us -> 135 us (level)
  starting transfers between devices: 41.6 us -> 40 us
    ppermute x25, starting transfers between devices: 41.5 us -> 39.9 us  [fetch(): return lax.ppermute(array, AXES, pairs)]
  transfers between devices with their start and end apart: 26 -> 26, of which waited for: 11 -> 11; matrix products, arithmetic and copies ran while one was open for 3% -> 3% of each run, Pallas kernels for 56% -> 57%
where the time goes in v3:
time: 135 us
  Pallas kernels  80.4 us (60%)
  starting transfers between devices  40 us (30%)
  waiting for transfers between devices  8.48 us (6%)
  local copies, waits for them, and re-layouts  5.41 us (4%)
    pallas_call x13, Pallas kernels, call(): pl.pallas_call(kernel, out_shape=out_shape, in_specs=[scalar_spec] * len(...  80.4 us
    ppermute x25, starting transfers between devices, fetch(): return lax.ppermute(array, AXES, pairs)  39.9 us
    ppermute x25, waiting for transfers between devices, fetch(): return lax.ppermute(array, AXES, pairs)  8.48 us
    unnamed x20, local copies, waits for them, and re-layouts  5.37 us
  transfers between devices with their start and end apart: 26, of which 11 were waited for; matrix products, arithmetic and copies ran while one was open for 3% of the time, Pallas kernels for 57%

profile of v3, /device:TPU:1, one launch (start us, length us, event | category | flops | bytes accessed | tf_op | source)
XLA Modules:
  0.0 134.7 jit_solution(13141834612873210870)
XLA Ops:
  0.0 3.3 %collective-permute-start = (bf16[48,1536]{1,0:T(8,128)(2,1)}, bf16[48,1536]{1,0:T(8,128)(2,1)}, u32[]{:S(2)}, u32[]{:S(2)}) collective-permute-start(bf16[48,1536]{1,0:T(8,128)(2,1)} %refs_0_), channel_id=1, source_target_pairs={{128,0},{129,1},{130,2},{131,3},{132,4},{133,5},{134,6},{135,7},{1... | collective-permute-start | bytes 442376 | tf_op jit(solution)/shard_map/tokens/ppermute | solution.py:40
  3.3 1.7 %collective-permute-start.2 = (bf16[48,1536]{1,0:T(8,128)(2,1)}, bf16[48,1536]{1,0:T(8,128)(2,1)}, u32[]{:S(2)}, u32[]{:S(2)}) collective-permute-start(bf16[48,1536]{1,0:T(8,128)(2,1)} %refs_0_), channel_id=1, source_target_pairs={{32,0},{33,1},{34,2},{35,3},{36,4},{37,5},{38,6},{39,7},{40,8},{41... | collective-permute-start | bytes 442376 | tf_op jit(solution)/shard_map/tokens/ppermute | solution.py:40
  5.0 1.5 %collective-permute-start.3 = (bf16[48,1536]{1,0:T(8,128)(2,1)}, bf16[48,1536]{1,0:T(8,128)(2,1)}, u32[]{:S(2)}, u32[]{:S(2)}) collective-permute-start(bf16[48,1536]{1,0:T(8,128)(2,1)} %refs_0_), channel_id=1, source_target_pairs={{64,0},{65,1},{66,2},{67,3},{68,4},{69,5},{70,6},{71,7},{72,8},{73... | collective-permute-start | bytes 442376 | tf_op jit(solution)/shard_map/project/ppermute | solution.py:40
  6.6 2.2 %copy.19 = bf16[192,8,2,384]{3,1,2,0:T(8,128)(2,1)S(1)} copy(bf16[192,8,2,384]{3,2,1,0:T(2,128)(2,1)} %bitcast.10) | data formatting | bytes 4718592
  11.4 2.8 %collective-permute-start.4 = (bf16[48,1536]{1,0:T(8,128)(2,1)}, bf16[48,1536]{1,0:T(8,128)(2,1)S(1)}, u32[]{:S(2)}, u32[]{:S(2)}) collective-permute-start(bf16[48,1536]{1,0:T(8,128)(2,1)} %collective-permute-done.refs_1_), channel_id=1, source_target_pairs={{64,0},{65,1},{66,2},{67,3},{68,4},{69,5},{70,6},{71,7},{72,8},{73... | collective-permute-start | bytes 442376 | tf_op jit(solution)/shard_map/project/ppermute | solution.py:40
  16.1 2.3 %project.1 = (bf16[3,64,384]{2,1,0:T(8,128)(2,1)S(1)}, bf16[3,128,384]{2,1,0:T(8,128)(2,1)S(1)}) custom-call(s32[1]{0:T(128)} %bitcast.3.high_ref, bf16[1536,576]{1,0:T(8,128)(2,1)S(1)} %halves.2.w_ref, f32[3,384]{1,0:T(4,128)S(1)} %copy-done.4, bf16[48,1536]{1,0:T(8,128)(2,1)S(1)} %copy-done.3, bf16[48,1536]{1,0:T(8,128)(2,1)} %collective-permute-done.refs_1_, ...), custom_call_target="tpu_custom_call" | custom-call | flops 679477248 | bytes 2953728 | tf_op jit(solution)/shard_map/project/project/pallas_call | solution.py:54
  18.4 1.7 %collective-permute-start.11 = (bf16[3,128,384]{2,1,0:T(8,128)(2,1)S(1)}, bf16[3,128,384]{2,1,0:T(8,128)(2,1)S(1)}, u32[]{:S(2)}, u32[]{:S(2)}) collective-permute-start(bf16[3,128,384]{2,1,0:T(8,128)(2,1)S(1)} %get-tuple-element.54.refs_4_), channel_id=1, source_target_pairs={{7,0},{0,1},{1,2},{2,3},{3,4},{4,5},{5,6},{6,7},{15,8},{8,9},{9,10... | collective-permute-start | bytes 884744 | tf_op jit(solution)/shard_map/exchange/ppermute | solution.py:40
  20.1 4.0 %collective-permute-start.7 = (bf16[3,128,384]{2,1,0:T(8,128)(2,1)S(1)}, bf16[3,128,384]{2,1,0:T(8,128)(2,1)S(1)}, u32[]{:S(2)}, u32[]{:S(2)}) collective-permute-start(bf16[3,128,384]{2,1,0:T(8,128)(2,1)S(1)} %get-tuple-element.54.refs_4_), channel_id=1, source_target_pairs={{1,0},{2,1},{3,2},{4,3},{5,4},{6,5},{7,6},{0,7},{9,8},{10,9},{11,1... | collective-permute-start | bytes 884744 | tf_op jit(solution)/shard_map/exchange/ppermute | solution.py:40
  24.1 2.7 %collective-permute-start.15 = (bf16[3,64,384]{2,1,0:T(8,128)(2,1)S(1)}, bf16[3,64,384]{2,1,0:T(8,128)(2,1)S(1)}, u32[]{:S(2)}, u32[]{:S(2)}) collective-permute-start(bf16[3,64,384]{2,1,0:T(8,128)(2,1)S(1)} %get-tuple-element.55.refs_0_), channel_id=1, source_target_pairs={{8,0},{9,1},{10,2},{11,3},{12,4},{13,5},{14,6},{15,7},{16,8},{17,9... | collective-permute-start | bytes 442376 | tf_op jit(solution)/shard_map/exchange/ppermute | solution.py:40
  26.9 1.6 %collective-permute-start.17 = (bf16[3,64,384]{2,1,0:T(8,128)(2,1)S(1)}, bf16[3,64,384]{2,1,0:T(8,128)(2,1)S(1)}, u32[]{:S(2)}, u32[]{:S(2)}) collective-permute-start(bf16[3,64,384]{2,1,0:T(8,128)(2,1)S(1)} %get-tuple-element.55.refs_0_), channel_id=1, source_target_pairs={{16,0},{17,1},{18,2},{19,3},{20,4},{21,5},{22,6},{23,7},{24,8},{25... | collective-permute-start | bytes 442376 | tf_op jit(solution)/shard_map/exchange/ppermute | solution.py:40
  28.5 2.7 %collective-permute-done.11.refs_6_ = bf16[3,128,384]{2,1,0:T(8,128)(2,1)S(1)} collective-permute-done((bf16[3,128,384]{2,1,0:T(8,128)(2,1)S(1)}, bf16[3,128,384]{2,1,0:T(8,128)(2,1)S(1)}, u32[]{:S(2)}, u32[]{:S(2)}) %collective-permute-start.11) | collective-permute-done | bytes 294944 | tf_op jit(solution)/shard_map/exchange/ppermute | solution.py:40
  31.2 2.7 %collective-permute-start.8 = (bf16[3,128,384]{2,1,0:T(8,128)(2,1)S(1)}, bf16[3,128,384]{2,1,0:T(8,128)(2,1)S(1)}, u32[]{:S(2)}, u32[]{:S(2)}) collective-permute-start(bf16[3,128,384]{2,1,0:T(8,128)(2,1)S(1)} %collective-permute-done.7.refs_5_), channel_id=1, source_target_pairs={{1,0},{2,1},{3,2},{4,3},{5,4},{6,5},{7,6},{0,7},{9,8},{10,9},{11,1... | collective-permute-start | bytes 884744 | tf_op jit(solution)/shard_map/exchange/ppermute | solution.py:40
  34.7 20.5 %attend_first.1 = (f32[3,80,1536]{2,1,0:T(8,128)S(1)}, f32[3,8,1536]{2,1,0:T(8,128)S(1)}, f32[8,128]{1,0:T(8,128)S(1)}, bf16[3,128,1536]{2,1,0:T(8,128)(2,1)S(1)}, f32[3,8,128]{2,1,0:T(8,128)S(1)}) custom-call(bf16[3,64,384]{2,1,0:T(8,128)(2,1)S(1)} %get-tuple-element.55.refs_0_, bf16[3,64,384]{2,1,0:T(8,128)(2,1)S(1)} %collective-permute-done.15.refs_1_, ...), custom_call_target="tpu_custom_call" | custom-call | flops 13271040000 | bytes 1474560 | tf_op jit(solution)/shard_map/attend/attend_first/pallas_call | solution.py:54
  55.3 2.7 %collective-permute-start.9 = (bf16[3,128,384]{2,1,0:T(8,128)(2,1)S(1)}, bf16[3,128,384]{2,1,0:T(8,128)(2,1)S(1)}, u32[]{:S(2)}, u32[]{:S(2)}) collective-permute-start(bf16[3,128,384]{2,1,0:T(8,128)(2,1)S(1)} %collective-permute-done.8.refs_0_), channel_id=1, source_target_pairs={{1,0},{2,1},{3,2},{4,3},{5,4},{6,5},{7,6},{0,7},{9,8},{10,9},{11,1... | collective-permute-start | bytes 884744 | tf_op jit(solution)/shard_map/exchange/ppermute | solution.py:40
  58.0 16.9 %attend_next.2 = (f32[3,80,1536]{2,1,0:T(8,128)S(1)}, f32[3,8,1536]{2,1,0:T(8,128)S(1)}, f32[8,128]{1,0:T(8,128)S(1)}) custom-call(bf16[3,128,384]{2,1,0:T(8,128)(2,1)S(1)} %collective-permute-done.8.refs_0_, bf16[3,128,384]{2,1,0:T(8,128)(2,1)S(1)} %collective-permute-done.12.refs_1_, ...), custom_call_target="tpu_custom_call", output_to_operand_aliasing={{0}: (4, {}), {1}: (5, {}), {2}: (6, {})} | custom-call | flops 8847360000 | bytes 3407872 | tf_op jit(solution)/shard_map/attend/attend_next/pallas_call | solution.py:54
  75.2 1.5 %collective-permute-start.14 = (bf16[3,64,384]{2,1,0:T(8,128)(2,1)S(1)}, bf16[3,64,384]{2,1,0:T(8,128)(2,1)S(1)}, u32[]{:S(2)}, u32[]{:S(2)}) collective-permute-start(bf16[3,64,384]{2,1,0:T(8,128)(2,1)S(1)} %slice.9), channel_id=1, source_target_pairs={{7,0},{0,1},{1,2},{2,3},{3,4},{4,5},{5,6},{6,7},{15,8},{8,9},{9,10... | collective-permute-start | bytes 442376 | tf_op jit(solution)/shard_map/exchange/ppermute | solution.py:40
  76.7 16.9 %attend_next.3 = (f32[3,80,1536]{2,1,0:T(8,128)S(1)}, f32[3,8,1536]{2,1,0:T(8,128)S(1)}, f32[8,128]{1,0:T(8,128)S(1)}) custom-call(bf16[3,128,384]{2,1,0:T(8,128)(2,1)S(1)} %collective-permute-done.9.refs_0_, bf16[3,128,384]{2,1,0:T(8,128)(2,1)S(1)} %collective-permute-done.13.refs_1_, ...), custom_call_target="tpu_custom_call", output_to_operand_aliasing={{0}: (4, {}), {1}: (5, {}), {2}: (6, {})} | custom-call | flops 8847360000 | bytes 3407872 | tf_op jit(solution)/shard_map/attend/attend_next/pallas_call | solution.py:54
  93.6 15.2 %attend_last.1 = (f32[3,80,384]{2,1,0:T(8,128)S(1)}, f32[3,8,384]{2,1,0:T(8,128)S(1)}, f32[8,128]{1,0:T(8,128)S(1)}, bf16[208,384]{1,0:T(8,128)(2,1)}, bf16[208,...) custom-call(bf16[3,64,384]{2,1,0:T(8,128)(2,1)S(1)} %collective-permute-done.10.k_ref, ...), custom_call_target="tpu_custom_call" | custom-call | flops 4423680000 | bytes 3112960 | tf_op jit(solution)/shard_map/attend/attend_last/pallas_call | solution.py:54
  109.3 2.2 %collective-permute-start.19 = (bf16[208,384]{1,0:T(8,128)(2,1)}, bf16[208,384]{1,0:T(8,128)(2,1)S(1)}, u32[]{:S(2)}, u32[]{:S(2)}) collective-permute-start(bf16[208,384]{1,0:T(8,128)(2,1)} %get-tuple-element.80), channel_id=1, source_target_pairs={{8,0},{9,1},{10,2},{11,3},{12,4},{13,5},{14,6},{15,7},{16,8},{17,9... | collective-permute-start | bytes 479240 | tf_op jit(solution)/shard_map/combine/ppermute | solution.py:40
  112.4 2.1 %copy.20 = bf16[192,8,2,384]{3,1,2,0:T(8,128)(2,1)S(1)} copy(bf16[192,8,2,384]{3,2,1,0:T(2,128)(2,1)} %bitcast.11) | data formatting | bytes 4718592
  117.0 3.9 %attend_text.1 = (f32[3,80,384]{2,1,0:T(8,128)S(1)}, f32[3,8,384]{2,1,0:T(8,128)S(1)}, f32[8,128]{1,0:T(8,128)S(1)}) custom-call(bf16[3,128,384]{2,1,0:T(8,128)(2,1)S(1)} %text_project.1.refs_0_, bf16[3,128,1536]{2,1,0:T(8,128)(2,1)S(1)} %copy-done.7, ...), custom_call_target="tpu_custom_call", output_to_operand_aliasing={{0}: (3, {}), {1}: (4, {}), {2}: (5, {})} | custom-call | flops 1105920000 | bytes 1896448 | tf_op jit(solution)/shard_map/text/attend_text/pallas_call | solution.py:54
  121.2 1.3 collective-permute-start.21
  122.9 2.3 %collective-permute-start.23 = (bf16[96,192]{1,0:T(8,128)(2,1)S(1)}, bf16[96,192]{1,0:T(8,128)(2,1)S(1)}, u32[]{:S(2)}, u32[]{:S(2)}) collective-permute-start(bf16[96,192]{1,0:T(8,128)(2,1)S(1)} %get-tuple-element.84), channel_id=1, source_target_pairs={{128,0},{129,1},{130,2},{131,3},{132,4},{133,5},{134,6},{135,7},{1... | collective-permute-start | bytes 110600 | tf_op jit(solution)/shard_map/output/ppermute | solution.py:40
  127.6 5.4 %collective-permute-start.25 = (bf16[48,1536]{1,0:T(8,128)(2,1)S(1)}, bf16[48,1536]{1,0:T(8,128)(2,1)S(1)}, u32[]{:S(2)}, u32[]{:S(2)}) collective-permute-start(bf16[48,1536]{1,0:T(8,128)(2,1)S(1)} %get-tuple-element.92), channel_id=1, source_target_pairs={{64,0},{65,1},{66,2},{67,3},{68,4},{69,5},{70,6},{71,7},{72,8},{73... | collective-permute-start | bytes 442376 | tf_op jit(solution)/shard_map/output/ppermute | solution.py:40
  (65 shorter events, 14.1 us)
Async XLA Ops:
  0.0 9.9 %collective-permute-start = (bf16[48,1536]{1,0:T(8,128)(2,1)}, bf16[48,1536]{1,0:T(8,128)(2,1)}, u32[]{:S(2)}, u32[]{:S(2)}) collective-permute-start(bf16[48,1536]{1,0:T(8,128)(2,1)} %refs_0_), channel_id=1, source_target_pairs={{128,0},{129,1},{130,2},{131,3},{132,4},{133,5},{134,6},{135,7},{1... | collective-permute-start | bytes 442376 | tf_op jit(solution)/shard_map/tokens/ppermute | solution.py:40
  3.3 7.5 %collective-permute-start.1 = (bf16[48,1536]{1,0:T(8,128)(2,1)}, bf16[48,1536]{1,0:T(8,128)(2,1)}, u32[]{:S(2)}, u32[]{:S(2)}) collective-permute-start(bf16[48,1536]{1,0:T(8,128)(2,1)} %refs_0_), channel_id=1, source_target_pairs={{160,0},{161,1},{162,2},{163,3},{164,4},{165,5},{166,6},{167,7},{1... | collective-permute-start | bytes 442376 | tf_op jit(solution)/shard_map/tokens/ppermute | solution.py:40
  3.3 8.1 %collective-permute-start.2 = (bf16[48,1536]{1,0:T(8,128)(2,1)}, bf16[48,1536]{1,0:T(8,128)(2,1)}, u32[]{:S(2)}, u32[]{:S(2)}) collective-permute-start(bf16[48,1536]{1,0:T(8,128)(2,1)} %refs_0_), channel_id=1, source_target_pairs={{32,0},{33,1},{34,2},{35,3},{36,4},{37,5},{38,6},{39,7},{40,8},{41... | collective-permute-start | bytes 442376 | tf_op jit(solution)/shard_map/tokens/ppermute | solution.py:40
  5.0 9.7 %collective-permute-start.3 = (bf16[48,1536]{1,0:T(8,128)(2,1)}, bf16[48,1536]{1,0:T(8,128)(2,1)}, u32[]{:S(2)}, u32[]{:S(2)}) collective-permute-start(bf16[48,1536]{1,0:T(8,128)(2,1)} %refs_0_), channel_id=1, source_target_pairs={{64,0},{65,1},{66,2},{67,3},{68,4},{69,5},{70,6},{71,7},{72,8},{73... | collective-permute-start | bytes 442376 | tf_op jit(solution)/shard_map/project/ppermute | solution.py:40
  11.4 4.0 %collective-permute-start.4 = (bf16[48,1536]{1,0:T(8,128)(2,1)}, bf16[48,1536]{1,0:T(8,128)(2,1)S(1)}, u32[]{:S(2)}, u32[]{:S(2)}) collective-permute-start(bf16[48,1536]{1,0:T(8,128)(2,1)} %collective-permute-done.refs_1_), channel_id=1, source_target_pairs={{64,0},{65,1},{66,2},{67,3},{68,4},{69,5},{70,6},{71,7},{72,8},{73... | collective-permute-start | bytes 442376 | tf_op jit(solution)/shard_map/project/ppermute | solution.py:40
  18.4 12.8 %collective-permute-start.11 = (bf16[3,128,384]{2,1,0:T(8,128)(2,1)S(1)}, bf16[3,128,384]{2,1,0:T(8,128)(2,1)S(1)}, u32[]{:S(2)}, u32[]{:S(2)}) collective-permute-start(bf16[3,128,384]{2,1,0:T(8,128)(2,1)S(1)} %get-tuple-element.54.refs_4_), channel_id=1, source_target_pairs={{7,0},{0,1},{1,2},{2,3},{3,4},{4,5},{5,6},{6,7},{15,8},{8,9},{9,10... | collective-permute-start | bytes 884744 | tf_op jit(solution)/shard_map/exchange/ppermute | solution.py:40
  20.1 11.1 %collective-permute-start.7 = (bf16[3,128,384]{2,1,0:T(8,128)(2,1)S(1)}, bf16[3,128,384]{2,1,0:T(8,128)(2,1)S(1)}, u32[]{:S(2)}, u32[]{:S(2)}) collective-permute-start(bf16[3,128,384]{2,1,0:T(8,128)(2,1)S(1)} %get-tuple-element.54.refs_4_), channel_id=1, source_target_pairs={{1,0},{2,1},{3,2},{4,3},{5,4},{6,5},{7,6},{0,7},{9,8},{10,9},{11,1... | collective-permute-start | bytes 884744 | tf_op jit(solution)/shard_map/exchange/ppermute | solution.py:40
  24.1 9.8 %collective-permute-start.15 = (bf16[3,64,384]{2,1,0:T(8,128)(2,1)S(1)}, bf16[3,64,384]{2,1,0:T(8,128)(2,1)S(1)}, u32[]{:S(2)}, u32[]{:S(2)}) collective-permute-start(bf16[3,64,384]{2,1,0:T(8,128)(2,1)S(1)} %get-tuple-element.55.refs_0_), channel_id=1, source_target_pairs={{8,0},{9,1},{10,2},{11,3},{12,4},{13,5},{14,6},{15,7},{16,8},{17,9... | collective-permute-start | bytes 442376 | tf_op jit(solution)/shard_map/exchange/ppermute | solution.py:40
  26.9 7.3 %collective-permute-start.16 = (bf16[3,64,384]{2,1,0:T(8,128)(2,1)S(1)}, bf16[3,64,384]{2,1,0:T(8,128)(2,1)S(1)}, u32[]{:S(2)}, u32[]{:S(2)}) collective-permute-start(bf16[3,64,384]{2,1,0:T(8,128)(2,1)S(1)} %get-tuple-element.55.refs_0_), channel_id=1, source_target_pairs={{24,0},{25,1},{26,2},{27,3},{28,4},{29,5},{30,6},{31,7},{0,8},{1,9... | collective-permute-start | bytes 442376 | tf_op jit(solution)/shard_map/exchange/ppermute | solution.py:40
  26.9 7.8 %collective-permute-start.17 = (bf16[3,64,384]{2,1,0:T(8,128)(2,1)S(1)}, bf16[3,64,384]{2,1,0:T(8,128)(2,1)S(1)}, u32[]{:S(2)}, u32[]{:S(2)}) collective-permute-start(bf16[3,64,384]{2,1,0:T(8,128)(2,1)S(1)} %get-tuple-element.55.refs_0_), channel_id=1, source_target_pairs={{16,0},{17,1},{18,2},{19,3},{20,4},{21,5},{22,6},{23,7},{24,8},{25... | collective-permute-start | bytes 442376 | tf_op jit(solution)/shard_map/exchange/ppermute | solution.py:40
  31.2 24.0 %collective-permute-start.12 = (bf16[3,128,384]{2,1,0:T(8,128)(2,1)S(1)}, bf16[3,128,384]{2,1,0:T(8,128)(2,1)S(1)}, u32[]{:S(2)}, u32[]{:S(2)}) collective-permute-start(bf16[3,128,384]{2,1,0:T(8,128)(2,1)S(1)} %collective-permute-done.11.refs_6_), channel_id=1, source_target_pairs={{7,0},{0,1},{1,2},{2,3},{3,4},{4,5},{5,6},{6,7},{15,8},{8,9},{9,10... | collective-permute-start | bytes 884744 | tf_op jit(solution)/shard_map/exchange/ppermute | solution.py:40
  31.2 24.1 %collective-permute-start.8 = (bf16[3,128,384]{2,1,0:T(8,128)(2,1)S(1)}, bf16[3,128,384]{2,1,0:T(8,128)(2,1)S(1)}, u32[]{:S(2)}, u32[]{:S(2)}) collective-permute-start(bf16[3,128,384]{2,1,0:T(8,128)(2,1)S(1)} %collective-permute-done.7.refs_5_), channel_id=1, source_target_pairs={{1,0},{2,1},{3,2},{4,3},{5,4},{6,5},{7,6},{0,7},{9,8},{10,9},{11,1... | collective-permute-start | bytes 884744 | tf_op jit(solution)/shard_map/exchange/ppermute | solution.py:40
  55.2 19.9 %collective-permute-start.13 = (bf16[3,128,384]{2,1,0:T(8,128)(2,1)S(1)}, bf16[3,128,384]{2,1,0:T(8,128)(2,1)S(1)}, u32[]{:S(2)}, u32[]{:S(2)}) collective-permute-start(bf16[3,128,384]{2,1,0:T(8,128)(2,1)S(1)} %collective-permute-done.12.refs_1_), channel_id=1, source_target_pairs={{7,0},{0,1},{1,2},{2,3},{3,4},{4,5},{5,6},{6,7},{15,8},{8,9},{9,10... | collective-permute-start | bytes 884744 | tf_op jit(solution)/shard_map/exchange/ppermute | solution.py:40
  55.3 19.7 %collective-permute-start.9 = (bf16[3,128,384]{2,1,0:T(8,128)(2,1)S(1)}, bf16[3,128,384]{2,1,0:T(8,128)(2,1)S(1)}, u32[]{:S(2)}, u32[]{:S(2)}) collective-permute-start(bf16[3,128,384]{2,1,0:T(8,128)(2,1)S(1)} %collective-permute-done.8.refs_0_), channel_id=1, source_target_pairs={{1,0},{2,1},{3,2},{4,3},{5,4},{6,5},{7,6},{0,7},{9,8},{10,9},{11,1... | collective-permute-start | bytes 884744 | tf_op jit(solution)/shard_map/exchange/ppermute | solution.py:40
  74.9 51.7 %collective-permute-start.24 = (bf16[384,1536]{1,0:T(8,128)(2,1)S(1)}, bf16[384,1536]{1,0:T(8,128)(2,1)S(1)}, u32[]{:S(2)}, u32[]{:S(2)}) collective-permute-start(bf16[384,1536]{1,0:T(8,128)(2,1)S(1)} %copy-done), channel_id=1, source_target_pairs={{0,128},{1,129},{2,130},{3,131},{4,132},{5,133},{6,134},{7,135},{8... | collective-permute-start | bytes 3538952 | tf_op jit(solution)/shard_map/attend/ppermute | solution.py:47
  75.1 18.6 %collective-permute-start.10 = (bf16[3,64,384]{2,1,0:T(8,128)(2,1)S(1)}, bf16[3,64,384]{2,1,0:T(8,128)(2,1)S(1)}, u32[]{:S(2)}, u32[]{:S(2)}) collective-permute-start(bf16[3,64,384]{2,1,0:T(8,128)(2,1)S(1)} %slice.8), channel_id=1, source_target_pairs={{1,0},{2,1},{3,2},{4,3},{5,4},{6,5},{7,6},{0,7},{9,8},{10,9},{11,1... | collective-permute-start | bytes 442376 | tf_op jit(solution)/shard_map/exchange/ppermute | solution.py:40
  75.2 18.4 %collective-permute-start.14 = (bf16[3,64,384]{2,1,0:T(8,128)(2,1)S(1)}, bf16[3,64,384]{2,1,0:T(8,128)(2,1)S(1)}, u32[]{:S(2)}, u32[]{:S(2)}) collective-permute-start(bf16[3,64,384]{2,1,0:T(8,128)(2,1)S(1)} %slice.9), channel_id=1, source_target_pairs={{7,0},{0,1},{1,2},{2,3},{3,4},{4,5},{5,6},{6,7},{15,8},{8,9},{9,10... | collective-permute-start | bytes 442376 | tf_op jit(solution)/shard_map/exchange/ppermute | solution.py:40
  108.8 12.1 %collective-permute-start.18 = (bf16[208,384]{1,0:T(8,128)(2,1)}, bf16[208,384]{1,0:T(8,128)(2,1)S(1)}, u32[]{:S(2)}, u32[]{:S(2)}) collective-permute-start(bf16[208,384]{1,0:T(8,128)(2,1)} %get-tuple-element.79), channel_id=1, source_target_pairs={{24,0},{25,1},{26,2},{27,3},{28,4},{29,5},{30,6},{31,7},{0,8},{1,9... | collective-permute-start | bytes 479240 | tf_op jit(solution)/shard_map/combine/ppermute | solution.py:40
  109.3 11.6 %collective-permute-start.19 = (bf16[208,384]{1,0:T(8,128)(2,1)}, bf16[208,384]{1,0:T(8,128)(2,1)S(1)}, u32[]{:S(2)}, u32[]{:S(2)}) collective-permute-start(bf16[208,384]{1,0:T(8,128)(2,1)} %get-tuple-element.80), channel_id=1, source_target_pairs={{8,0},{9,1},{10,2},{11,3},{12,4},{13,5},{14,6},{15,7},{16,8},{17,9... | collective-permute-start | bytes 479240 | tf_op jit(solution)/shard_map/combine/ppermute | solution.py:40
  111.5 9.4 %collective-permute-start.20 = (bf16[208,384]{1,0:T(8,128)(2,1)S(1)}, bf16[208,384]{1,0:T(8,128)(2,1)S(1)}, u32[]{:S(2)}, u32[]{:S(2)}) collective-permute-start(bf16[208,384]{1,0:T(8,128)(2,1)S(1)} %get-tuple-element.81), channel_id=1, source_target_pairs={{16,0},{17,1},{18,2},{19,3},{20,4},{21,5},{22,6},{23,7},{24,8},{25... | collective-permute-start | bytes 479240 | tf_op jit(solution)/shard_map/combine/ppermute | solution.py:40
  121.2 4.5 %collective-permute-start.21 = (bf16[96,192]{1,0:T(8,128)(2,1)S(1)}, bf16[96,192]{1,0:T(8,128)(2,1)S(1)}, u32[]{:S(2)}, u32[]{:S(2)}) collective-permute-start(bf16[96,192]{1,0:T(8,128)(2,1)S(1)} %get-tuple-element.82), channel_id=1, source_target_pairs={{32,0},{33,1},{34,2},{35,3},{36,4},{37,5},{38,6},{39,7},{40,8},{41... | collective-permute-start | bytes 110600 | tf_op jit(solution)/shard_map/output/ppermute | solution.py:40
  122.5 4.2 %collective-permute-start.22 = (bf16[96,192]{1,0:T(8,128)(2,1)S(1)}, bf16[96,192]{1,0:T(8,128)(2,1)S(1)}, u32[]{:S(2)}, u32[]{:S(2)}) collective-permute-start(bf16[96,192]{1,0:T(8,128)(2,1)S(1)} %get-tuple-element.83), channel_id=1, source_target_pairs={{160,0},{161,1},{162,2},{163,3},{164,4},{165,5},{166,6},{167,7},{1... | collective-permute-start | bytes 110600 | tf_op jit(solution)/shard_map/output/ppermute | solution.py:40
  122.9 3.8 %collective-permute-start.23 = (bf16[96,192]{1,0:T(8,128)(2,1)S(1)}, bf16[96,192]{1,0:T(8,128)(2,1)S(1)}, u32[]{:S(2)}, u32[]{:S(2)}) collective-permute-start(bf16[96,192]{1,0:T(8,128)(2,1)S(1)} %get-tuple-element.84), channel_id=1, source_target_pairs={{128,0},{129,1},{130,2},{131,3},{132,4},{133,5},{134,6},{135,7},{1... | collective-permute-start | bytes 110600 | tf_op jit(solution)/shard_map/output/ppermute | solution.py:40
  127.6 6.4 %collective-permute-start.25 = (bf16[48,1536]{1,0:T(8,128)(2,1)S(1)}, bf16[48,1536]{1,0:T(8,128)(2,1)S(1)}, u32[]{:S(2)}, u32[]{:S(2)}) collective-permute-start(bf16[48,1536]{1,0:T(8,128)(2,1)S(1)} %get-tuple-element.92), channel_id=1, source_target_pairs={{64,0},{65,1},{66,2},{67,3},{68,4},{69,5},{70,6},{71,7},{72,8},{73... | collective-permute-start | bytes 442376 | tf_op jit(solution)/shard_map/output/ppermute | solution.py:40
  (11 other events, 86.7 us)
